TPU v7x, 128 devices: a whole 4x4x4 slice. The times are simulated.
128 devices in a mesh: row: 16 (over y, z_hi, core), col: 8 (over x, z_lo).
Axes of the slice: x: 4, y: 4, z: 4 (z_hi: 2, z_lo: 2; z = z_hi * 2 + z_lo), core: 2. Of those that a mesh axis runs over, the one named last changes fastest.
Arguments:
- diag_block: float32 [512, 512], P('row', 'col'), may hold values from 0 to 2.5, as said below
- panel_below: float32 [49152, 512], P('row', 'col'), may hold values from -1.8 to 1.8
- trailing: float32 [49152, 6144], P('row', 'col'), may hold values from -6 to 6
Outputs:
- diag_factor: float32 [512, 512], P('row', 'col')
- panel_factor: float32 [49152, 512], P('row', 'col')
- new_trailing: float32 [49152, 6144], P('row', 'col')
Inputs may be any that keep to these rules, and one draw needn't show every extreme that they name: `diag_block`: taken to matrix order in both dimensions, the block is symmetric with all eigenvalues 0.5 or more.
All inputs are finite; a program needn't handle non-finite values.
Results may differ from a plain program's by a relative error of at most 0.00015.
Values sent between devices are 32-bit elements; how exact they have to be, the bound alone decides.
No kernel may reach another device: no remote copies, remote signals or barrier semaphores. Data moves between devices by JAX's collectives and lax.ppermute only.
A program may use at most 128 MiB of HBM per device.

v0:
```python
import functools

import jax
import jax.numpy as jnp
from jax import lax
from jax.experimental import pallas as pl
from jax.experimental.pallas import tpu as pltpu
from jax.sharding import Mesh
from jax.sharding import PartitionSpec as P

HI = lax.Precision.HIGHEST
WIDTH = 512
BLK = 128
SUB = 8


def dot(a, b, ca, cb, precision=HI):
    return lax.dot_general(
        a, b, (((ca,), (cb,)), ((), ())), precision=precision, preferred_element_type=jnp.float32
    )


def lanes_of(x, k):
    return jnp.broadcast_to(x[:, k : k + 1], (SUB, BLK))


def row_of(x, j):
    return jnp.broadcast_to(x[j : j + 1, :], (SUB, BLK))


def eliminate_strip(rows, first):
    lane = lax.broadcasted_iota(jnp.int32, (SUB, BLK), 1)
    sub = lax.broadcasted_iota(jnp.int32, (SUB, BLK), 0)
    rows, scales, ahead = list(rows), [], None
    for b in range(len(rows)):
        base = SUB * (first + b)
        cols = {
            i: [lanes_of(rows[i], base + k) for k in range(SUB)]
            for i in range(b, len(rows))
            if i > b or ahead is None
        }
        if ahead is not None:
            cols[b] = ahead
        if b + 1 < len(rows):
            ahead = [lanes_of(rows[b + 1], base + SUB + k) for k in range(SUB)]
        scale = jnp.zeros((SUB, BLK), jnp.float32)
        for j in range(SUB):
            pivot_row = {k: row_of(cols[b][k], j) for k in range(j, SUB)}
            at = lane == base + j
            wide = jnp.where(at, 1.0, row_of(rows[b], j))
            inv = 1.0 / pivot_row[j]
            scale = jnp.where(sub == j, lax.rsqrt(pivot_row[j]), scale)
            for i in range(b, len(rows)):
                m = cols[i][j] * inv
                here = at
                if i == b:
                    m = jnp.where(sub > j, m, 0.0)
                    here = at & (sub > j)
                if i == b + 1:
                    for k in range(SUB):
                        ahead[k] = ahead[k] - m * row_of(cols[i][j], k)
                for k in range(j + 1, SUB):
                    cols[i][k] = cols[i][k] - m * pivot_row[k]
                rows[i] = jnp.where(here, 0.0, rows[i]) - m * wide
        rows[b] = rows[b] * scale
        scales.append(scale)
    return rows, scales


def eliminate(rows, strip=8):
    lane = lax.broadcasted_iota(jnp.int32, (SUB, BLK), 1)
    sub = lax.broadcasted_iota(jnp.int32, (SUB, BLK), 0)
    rows, scales = list(rows), []
    for s in range(0, len(rows), strip):
        e = s + strip
        rows[s:e], found = eliminate_strip(rows[s:e], s)
        scales += found
        if e < len(rows):
            inside = (lane >= SUB * s) & (lane < SUB * e)
            own = [
                jnp.where(
                    inside & (lane >= sub + SUB * i),
                    jnp.where(lane == sub + SUB * i, scales[i], 0.0),
                    rows[i],
                )
                for i in range(s, e)
            ]
            change = dot(jnp.concatenate(rows[s:e], axis=0), jnp.concatenate(own, axis=0), 0, 0)
            for i in range(e, len(rows)):
                rows[i] = jnp.where(inside, 0.0, rows[i]) - change[SUB * i : SUB * i + SUB]
    return rows, scales


def fill(tall_ref, start, stride, value):
    rows, columns = value.shape
    height = tall_ref.shape[0] * BLK // columns
    for i in range(columns // BLK):
        tall_ref[pl.ds(i * height + start, rows, stride=stride), :] = value[:, BLK * i : BLK * i + BLK]


def pick(tall_ref, start, stride, rows, columns, height):
    return jnp.concatenate(
        [
            tall_ref[pl.ds(i * height + start, rows, stride=stride), :]
            for i in range(columns // BLK)
        ],
        axis=1,
    )


def lay(tall_ref, value):
    height = value.shape[0]
    for i in range(value.shape[1] // BLK):
        tall_ref[i * height : i * height + height, :] = value[:, BLK * i : BLK * i + BLK]


def assemble(mine_ref, other_ref, wide_ref, tall_ref, a_ref):
    core = lax.axis_index("core")
    left = lax.broadcasted_iota(jnp.int32, (16, BLK), 1) < BLK // 2
    for ref, start in ((mine_ref, core), (other_ref, 1 - core)):
        for yz in range(8):
            for x in range(4):
                one, two = ref[yz * 8 + 2 * x], ref[yz * 8 + 2 * x + 1]
                upper = jnp.where(left, one, pltpu.roll(two, BLK // 2, 1))
                lower = jnp.where(left, pltpu.roll(one, BLK // 2, 1), two)
                at = x * WIDTH + yz * 2 + start
                wide_ref[pl.ds(at, 16, stride=16), :] = upper
                wide_ref[pl.ds(at + WIDTH // 2, 16, stride=16), :] = lower
    for x in range(4):
        turned = wide_ref[x * WIDTH : x * WIDTH + WIDTH, :].T
        fill(tall_ref, 2 * x, 8, turned[:64])
        fill(tall_ref, 2 * x + 1, 8, turned[64:])
    for i in range(4):
        a_ref[:, BLK * i : BLK * i + BLK] = tall_ref[i * WIDTH : i * WIDTH + WIDTH, :]


def factor_steps(offsets, r_ref, u_ref, m_ref, t_ref):
    lane = lax.broadcasted_iota(jnp.int32, (SUB, BLK), 1)
    sub = lax.broadcasted_iota(jnp.int32, (SUB, BLK), 0)
    for o in offsets:
        e = o + BLK
        rows = [r_ref[o + i : o + i + SUB, o:e] for i in range(0, BLK, SUB)]
        rows, scales = eliminate(rows)
        for i in range(BLK // SUB):
            at = sub + SUB * i
            u_ref[o + SUB * i : o + SUB * i + SUB, o:e] = jnp.where(lane >= at, rows[i], 0.0)
            t_ref[SUB * i : SUB * i + SUB, :] = jnp.where(
                lane < at, rows[i], jnp.where(lane == at, scales[i], 0.0)
            )
        inv = t_ref[...]
        m_ref[o:e, o:e] = inv
        if o:
            m_ref[o:e, :o] = dot(inv, r_ref[o:e, :o], 1, 0)
        if e < WIDTH:
            u = dot(inv, r_ref[o:e, e:], 1, 0)
            u_ref[o:e, e:] = u
            r_ref[e:, e:] = r_ref[e:, e:] - dot(u, u, 0, 0)
            z = dot(u, m_ref[o:e, :e], 0, 0)
            if o:
                r_ref[e:, :o] = r_ref[e:, :o] - z[:, :o]
            r_ref[e:, o:e] = -z[:, o:]


VMEM = pl.BlockSpec(memory_space=pltpu.VMEM)


def cost(flops, bytes_accessed):
    return pl.CostEstimate(flops=flops, bytes_accessed=bytes_accessed, transcendentals=0)


PLACES = ((0, 0), (0, 1), (3, 0), (1, 0), (1, 1), (3, 1), (2, 0), (2, 1))


def weights_kernel(
    mine_ref, other_ref, p0_ref, p1_ref, p2_ref, p3_ref, d_ref, own_ref, w_ref,
    r_ref, u_ref, m_ref, b_ref, wide_ref, t_ref, k_ref, p_ref,
):
    assemble(mine_ref, other_ref, wide_ref, t_ref, r_ref)
    u_ref[...] = jnp.zeros_like(u_ref)
    m_ref[...] = jnp.zeros_like(m_ref)
    factor_steps(range(0, WIDTH, BLK), r_ref, u_ref, m_ref, b_ref)
    y, zh, core = lax.axis_index("y"), lax.axis_index("zh"), lax.axis_index("core")
    x, zl = lax.axis_index("x"), lax.axis_index("zl")
    col, row = x * 2 + zl, (y * 2 + zh) * 2 + core
    half = WIDTH // 8
    lay(t_ref, m_ref[...].T)
    arrived = [2 * ((x + dx) % 4) + (zl + dz) % 2 for dx, dz in PLACES]
    for i in range(8):
        c = 2 * ((y + 4 - i // 2) % 4) + (zh + i % 2) % 2
        k_ref[half * i : half * i + half, :] = pick(t_ref, c, 8, half, WIDTH, WIDTH)
    for i, c in enumerate(arrived):
        p_ref[half * i : half * i + half, :] = pick(t_ref, c, 8, half, WIDTH, WIDTH)
    top = jnp.concatenate(
        [ref[i] for ref in (p0_ref, p1_ref, p2_ref, p3_ref) for i in range(2)], axis=0
    )
    solved = dot(top, k_ref[...], 0, 0)
    w_ref[...] = dot(solved, p_ref[...], 1, 1)
    lay(t_ref, m_ref[...])
    mine = pick(t_ref, col, 8, half, WIDTH, WIDTH)
    lay(t_ref, u_ref[...])
    both = jnp.concatenate([mine, pick(t_ref, col, 8, half, WIDTH, WIDTH)], axis=0).T
    t_ref[:WIDTH, :] = both
    own = jnp.concatenate([t_ref[pl.ds(c, half, stride=8), :] for c in arrived], axis=0)
    own_ref[...] = own[:, :half].T
    d_ref[...] = t_ref[pl.ds(row, WIDTH // 16, stride=16), :][:, half:]


def make_weights(mine, other, pairs):
    square, tall = pltpu.VMEM((WIDTH, WIDTH), jnp.float32), pltpu.VMEM((4 * WIDTH, BLK), jnp.float32)
    return pl.pallas_call(
        weights_kernel,
        out_shape=[
            jax.ShapeDtypeStruct((WIDTH // 16, WIDTH // 8), jnp.float32),
            jax.ShapeDtypeStruct((WIDTH // 8, WIDTH), jnp.float32),
            jax.ShapeDtypeStruct((pairs[0].shape[2], WIDTH), jnp.float32),
        ],
        in_specs=[VMEM] * 6,
        out_specs=[VMEM] * 3,
        scratch_shapes=[square] * 3
        + [pltpu.VMEM((BLK, BLK), jnp.float32), tall, tall, square, square],
        cost_estimate=cost(3 * 10**10, 10**6),
        compiler_params=pltpu.CompilerParams(vmem_limit_bytes=24 << 20),
        name="weights",
    )(mine, other, *pairs)


def split(a):
    high = a.astype(jnp.bfloat16)
    return high, (a - high.astype(jnp.float32)).astype(jnp.bfloat16)


def thrice(a, b, ca, cb):
    (ah, al), (bh, bl) = a, b
    return dot(ah, bh, ca, cb, None) + dot(ah, bl, ca, cb, None) + dot(al, bh, ca, cb, None)


def subtract(place, own, high, low, blocks, trail_ref, pf, pf_ref, out_ref):
    part = jnp.concatenate([ref[...] for ref in blocks], axis=0)
    at = slice(WIDTH // 8 * place, WIDTH // 8 * place + part.shape[0])
    mine = thrice(split(own[:, at]), split(part), 1, 0)
    pf_ref[...] = mine if pf is None else pf[...] + mine
    (ah, al), bh, bl = split(part.T), high[at, :], low[at, :]
    if 3 * part.shape[0] <= 256:
        change = dot(
            jnp.concatenate([ah, al, ah], axis=1), jnp.concatenate([bh, bh, bl], axis=0), 1, 0, None
        )
    else:
        change = thrice((ah, al), (bh, bl), 1, 0)
    out_ref[...] = trail_ref[...] - change


def start_kernel(mine_ref, other_ref, own_ref, *refs):
    blocks, (trail_ref, pf_ref, out_ref, high_ref, low_ref, w_ref) = refs[:-6], refs[-6:]

    @pl.when(pl.program_id(0) == 0)
    def _():
        core = lax.axis_index("core")
        n = mine_ref.shape[0]
        fill(w_ref, core, 2, mine_ref[...])
        fill(w_ref, 1 - core, 2, other_ref[...])
        for i in range(WIDTH // BLK):
            at = slice(BLK * i, BLK * i + BLK)
            high_ref[at, :], low_ref[at, :] = split(w_ref[2 * n * i : 2 * n * i + 2 * n, :].T)

    subtract(0, own_ref[...], high_ref, low_ref, blocks, trail_ref, None, pf_ref, out_ref)


def go_on_kernel(own_ref, high_ref, low_ref, *refs, place):
    blocks, (pf_in_ref, trail_ref, pf_ref, out_ref) = refs[:-4], refs[-4:]
    subtract(place, own_ref[...], high_ref, low_ref, blocks, trail_ref, pf_in_ref, pf_ref, out_ref)


def whole(shape):
    return pl.BlockSpec(shape, lambda i: (0, 0))


def update_start(mine, other, own, blocks, trailing, tile=256):
    rows, columns = trailing.shape
    lanes = pl.BlockSpec((WIDTH // 8, tile), lambda i: (0, i))
    wide = pl.BlockSpec((tile, columns), lambda i: (i, 0))
    return pl.pallas_call(
        start_kernel,
        grid=(rows // tile,),
        out_shape=[
            jax.ShapeDtypeStruct((WIDTH // 8, rows), jnp.float32),
            jax.ShapeDtypeStruct((rows, columns), jnp.float32),
        ]
        + [jax.ShapeDtypeStruct((WIDTH, columns), jnp.bfloat16)] * 2,
        in_specs=[whole(mine.shape), whole(other.shape), whole(own.shape)] + [lanes] * len(blocks)
        + [wide],
        out_specs=[lanes, wide] + [whole((WIDTH, columns))] * 2,
        scratch_shapes=[pltpu.VMEM((columns * WIDTH // BLK, BLK), jnp.float32)],
        cost_estimate=cost(8 * 10**9, 10**7),
        compiler_params=pltpu.CompilerParams(vmem_limit_bytes=20 << 20),
        name="update_start",
    )(mine, other, own, *blocks, trailing)


def update_more(place, own, high, low, blocks, pf, trailing, tile, name):
    rows, columns = trailing.shape
    lanes = pl.BlockSpec((WIDTH // 8, tile), lambda i: (0, i))
    wide = pl.BlockSpec((tile, columns), lambda i: (i, 0))
    return pl.pallas_call(
        functools.partial(go_on_kernel, place=place),
        grid=(rows // tile,),
        out_shape=[
            jax.ShapeDtypeStruct((WIDTH // 8, rows), jnp.float32),
            jax.ShapeDtypeStruct((rows, columns), jnp.float32),
        ],
        in_specs=[whole(own.shape), whole(high.shape), whole(low.shape)]
        + [lanes] * (len(blocks) + 1)
        + [wide],
        out_specs=[lanes, wide],
        cost_estimate=cost(10**9 * len(blocks), 10**7),
        compiler_params=pltpu.CompilerParams(vmem_limit_bytes=16 << 20),
        name=name,
    )(own, high, low, *blocks, pf, trailing)


def ring(n, step):
    return [(i, (i + step) % n) for i in range(n)]


def shift(x, axis, step):
    return lax.ppermute(x, axis, ring(lax.axis_size(axis), step))


def order(*arrays):
    return lax.optimization_barrier(arrays)


def gather_tiles(tile):
    half = tile.shape[0] // 2
    flat = jnp.concatenate([tile[:half], tile[half:]], axis=1)
    return lax.all_to_all(
        jnp.broadcast_to(flat[None], (64,) + flat.shape), ("y", "zh", "x", "zl"), 0, 0, tiled=True
    )


def top_moves(flip):
    moves = []
    for source in range(128):
        y, zh, core, x, zl = (source // s % n for s, n in ((32, 4), (16, 2), (8, 2), (2, 4), (1, 2)))
        target = (((x * 2 + (zl + flip) % 2) * 2 + y // 2) * 4 + 2 * (y % 2) + zh) * 2 + core
        moves.append((source, target))
    return moves


def shards(diag_block, panel_below, trailing):
    panel_t = panel_below.T
    top_len = trailing.shape[1] // 2
    everything = ("y", "zh", "core", "x", "zl")
    raw = panel_t[:, :top_len]
    pieces = [lax.ppermute(raw, everything, top_moves(flip)) for flip in (0, 1)]
    diag_block, *pieces = order(diag_block, *pieces)
    from_z = shift(panel_t, "zl", 1)
    from_l = shift(panel_t, "x", 1)
    from_r = shift(panel_t, "x", -1)
    mine = gather_tiles(diag_block)
    head = BLK
    ahead = shift(from_r[:, :head], "x", -1)
    ahead, *pieces = order(ahead, *pieces)
    pair = jnp.stack(pieces)
    pairs = [pair] + [shift(pair, "y", s) for s in (1, 2, 3)]
    other = shift(mine, "core", 1)
    mine, other, from_z, from_l, from_r, ahead = order(mine, other, from_z, from_l, from_r, ahead)
    from_rz = shift(from_r, "zl", 1)
    from_lz = shift(from_z, "x", 1)
    from_2 = jnp.concatenate([ahead, shift(from_r[:, head:], "x", -1)], axis=1)
    diag_factor, own, weights = make_weights(mine, other, pairs)
    weights, from_rz, from_lz, from_2 = order(weights, from_rz, from_lz, from_2)
    weights_other = shift(weights, "core", 1)
    third = panel_t.shape[1] // 3
    parts = (
        shift(from_2[:, :third], "zl", 1),
        shift(from_lz[:, third : 2 * third], "x", 1),
        shift(from_rz[:, 2 * third :], "x", -1),
    )
    blocks = [panel_t, from_z, from_l, from_r, from_rz, from_lz, from_2]
    factor_part, rest, high, low = update_start(weights, weights_other, own, blocks, trailing)
    factor_part, rest, *parts = order(factor_part, rest, *parts)
    from_2z = jnp.concatenate(parts, axis=1)
    panel_factor, new_trailing = update_more(
        7, own, high, low, [from_2z], factor_part, rest, 512, "update_last"
    )
    return (diag_factor, panel_factor.T, new_trailing)


def solution(mesh):
    fine = Mesh(mesh.devices.reshape(4, 2, 2, 4, 2), ("y", "zh", "core", "x", "zl"))
    spec = P(("y", "zh", "core"), ("x", "zl"))
    return jax.shard_map(
        shards, mesh=fine, in_specs=(spec,) * 3, out_specs=(spec,) * 3, check_vma=False
    )
```

profile of v0, /device:TPU:1, one launch (start us, length us, event | category | flops | bytes accessed | tf_op | source)
XLA Modules:
  0.0 104.7 jit_solution(1691118533882537201)
XLA Ops:
  0.6 0.9 slice.32
  1.5 5.1 %collective-permute-start.1 = (f32[64,384]{1,0:T(8,128)S(1)}, f32[64,384]{1,0:T(8,128)S(1)}, u32[]{:S(2)}, u32[]{:S(2)}) collective-permute-start(f32[64,384]{1,0:T(8,128)S(1)} %slice.32), channel_id=1, source_target_pairs={{0,16},{1,0},{2,48},{3,32},{4,80},{5,64},{6,112},{7,96},{8,17},{9,... | collective-permute-start | bytes 294920 | tf_op jit(solution)/shard_map/ppermute | solution.py:354
  6.7 1.9 %collective-permute-start = (f32[64,384]{1,0:T(8,128)S(1)}, f32[64,384]{1,0:T(8,128)S(1)}, u32[]{:S(2)}, u32[]{:S(2)}) collective-permute-start(f32[64,384]{1,0:T(8,128)S(1)} %slice.32), channel_id=1, source_target_pairs={{0,0},{1,16},{2,32},{3,48},{4,64},{5,80},{6,96},{7,112},{8,1},{9,1... | collective-permute-start | bytes 294920 | tf_op jit(solution)/shard_map/ppermute | solution.py:354
  8.6 4.9 %collective-permute-start.5 = (f32[64,3072]{1,0:T(8,128)}, f32[64,3072]{1,0:T(8,128)S(1)}, u32[]{:S(2)}, u32[]{:S(2)}) collective-permute-start(f32[64,3072]{1,0:T(8,128)} %bitcast.5), channel_id=1, source_target_pairs={{0,6},{2,0},{4,2},{6,4},{1,7},{3,1},{5,3},{7,5},{8,14},{10,8},{12,... | collective-permute-start | bytes 2359304 | tf_op jit(solution)/shard_map/ppermute | solution.py:325
  13.5 0.0 collective-permute-done.1
  13.5 0.7 collective-permute-done
  14.2 0.7 fusion
  14.9 0.1 pad_maximum_fusion.3
  15.0 0.8 broadcast_in_dim.2
  15.8 13.6 %all-to-all-start = ((f32[64,16,128]{2,1,0:T(8,128)}), f32[64,16,128]{2,1,0:T(8,128)S(1)}, u32[]{:S(2)}, u32[]{:S(2)}) async-start(f32[64,16,128]{2,1,0:T(8,128)} %broadcast_in_dim.2), calls=%async_computation | async-start | bytes 1048576 | tf_op jit(solution)/shard_map/all_to_all | solution.py:335
  29.4 1.1 %collective-permute-start.4 = (f32[64,3072]{1,0:T(8,128)}, f32[64,3072]{1,0:T(8,128)S(1)}, u32[]{:S(2)}, u32[]{:S(2)}) collective-permute-start(f32[64,3072]{1,0:T(8,128)} %bitcast.6), channel_id=1, source_target_pairs={{0,2},{2,4},{4,6},{6,0},{1,3},{3,5},{5,7},{7,1},{8,10},{10,12},{12... | collective-permute-start | bytes 2359304 | tf_op jit(solution)/shard_map/ppermute | solution.py:325
  30.5 1.2 %collective-permute-start.3 = (f32[64,3072]{1,0:T(8,128)}, f32[64,3072]{1,0:T(8,128)S(1)}, u32[]{:S(2)}, u32[]{:S(2)}) collective-permute-start(f32[64,3072]{1,0:T(8,128)} %bitcast.7), channel_id=1, source_target_pairs={{0,1},{1,0},{2,3},{3,2},{4,5},{5,4},{6,7},{7,6},{8,9},{9,8},{10,11... | collective-permute-start | bytes 2359304 | tf_op jit(solution)/shard_map/ppermute | solution.py:325
  31.7 10.1 %all-to-all-done.mine_ref = f32[64,16,128]{2,1,0:T(8,128)S(1)} async-done(((f32[64,16,128]{2,1,0:T(8,128)}), f32[64,16,128]{2,1,0:T(8,128)S(1)}, u32[]{:S(2)}, u32[]{:S(2)}) %all-to-all-start) | async-done | bytes 524320 | tf_op jit(solution)/shard_map/all_to_all | solution.py:335
  41.8 2.8 %collective-permute-start.2 = (f32[64,16,128]{2,1,0:T(8,128)S(1)}, f32[64,16,128]{2,1,0:T(8,128)S(1)}, u32[]{:S(2)}, u32[]{:S(2)}) collective-permute-start(f32[64,16,128]{2,1,0:T(8,128)S(1)} %all-to-all-done.mine_ref), channel_id=1, source_target_pairs={{0,8},{8,0},{1,9},{9,1},{2,10},{10,2},{3,11},{11,3},{4,12},{12,4},... | collective-permute-start | bytes 1572872 | tf_op jit(solution)/shard_map/ppermute | solution.py:325
  44.6 0.0 collective-permute-done.5.refs_3_
  44.7 1.9 %collective-permute-start.6 = (f32[64,128]{1,0:T(8,128)S(1)}, f32[64,128]{1,0:T(8,128)S(1)}, u32[]{:S(2)}, u32[]{:S(2)}) collective-permute-start(f32[64,128]{1,0:T(8,128)S(1)} %slice.33), channel_id=1, source_target_pairs={{0,6},{2,0},{4,2},{6,4},{1,7},{3,1},{5,3},{7,5},{8,14},{10,8},{12,... | collective-permute-start | bytes 98312 | tf_op jit(solution)/shard_map/ppermute | solution.py:325
  46.5 1.3 %collective-permute-done.6 = f32[64,128]{1,0:T(8,128)S(1)} collective-permute-done((f32[64,128]{1,0:T(8,128)S(1)}, f32[64,128]{1,0:T(8,128)S(1)}, u32[]{:S(2)}, u32[]{:S(2)}) %collective-permute-start.6) | collective-permute-done | bytes 32800 | tf_op jit(solution)/shard_map/ppermute | solution.py:325
  47.8 1.0 collective-permute-start.9
  48.8 1.6 %collective-permute-start.8 = (f32[2,64,384]{2,1,0:T(8,128)S(1)}, f32[2,64,384]{2,1,0:T(8,128)S(1)}, u32[]{:S(2)}, u32[]{:S(2)}) collective-permute-start(f32[2,64,384]{2,1,0:T(8,128)S(1)} %pad_maximum_fusion.2.p0_ref), channel_id=1, source_target_pairs={{0,64},{32,96},{64,0},{96,32},{1,65},{33,97},{65,1},{97,33},{2,66}... | collective-permute-start | bytes 589832 | tf_op jit(solution)/shard_map/ppermute | solution.py:325
  50.5 4.0 %collective-permute-done.4.refs_2_ = f32[64,3072]{1,0:T(8,128)S(1)} collective-permute-done((f32[64,3072]{1,0:T(8,128)}, f32[64,3072]{1,0:T(8,128)S(1)}, u32[]{:S(2)}, u32[]{:S(2)}) %collective-permute-start.4) | collective-permute-done | bytes 786464 | tf_op jit(solution)/shard_map/ppermute | solution.py:325
  54.5 1.2 %collective-permute-start.7 = (f32[2,64,384]{2,1,0:T(8,128)S(1)}, f32[2,64,384]{2,1,0:T(8,128)S(1)}, u32[]{:S(2)}, u32[]{:S(2)}) collective-permute-start(f32[2,64,384]{2,1,0:T(8,128)S(1)} %pad_maximum_fusion.2.p0_ref), channel_id=1, source_target_pairs={{0,32},{32,64},{64,96},{96,0},{1,33},{33,65},{65,97},{97,1},{2,34}... | collective-permute-start | bytes 589832 | tf_op jit(solution)/shard_map/ppermute | solution.py:325
  55.7 0.0 collective-permute-done.3.refs_1_
  55.7 0.0 collective-permute-done.2.other_ref
  55.7 0.1 slice.28
  55.8 0.0 copy-start
  55.8 0.0 slice-start.1
  55.8 0.0 slice-start.2
  55.8 1.3 %collective-permute-start.10 = (f32[64,3072]{1,0:T(8,128)S(1)}, f32[64,3072]{1,0:T(8,128)S(1)}, u32[]{:S(2)}, u32[]{:S(2)}) collective-permute-start(f32[64,3072]{1,0:T(8,128)S(1)} %collective-permute-done.5.refs_3_), channel_id=1, source_target_pairs={{0,1},{1,0},{2,3},{3,2},{4,5},{5,4},{6,7},{7,6},{8,9},{9,8},{10,11... | collective-permute-start | bytes 2359304 | tf_op jit(solution)/shard_map/ppermute | solution.py:325
  57.1 0.6 collective-permute-start.12
  57.7 0.0 collective-permute-done.9.p3_ref
  57.7 0.9 collective-permute-start.11
  58.6 0.0 collective-permute-done.8.p2_ref
  58.6 2.4 %collective-permute-done.7.p1_ref = f32[2,64,384]{2,1,0:T(8,128)S(1)} collective-permute-done((f32[2,64,384]{2,1,0:T(8,128)S(1)}, f32[2,64,384]{2,1,0:T(8,128)S(1)}, u32[]{:S(2)}, u32[]{:S(2)}) %collective-permute-start.7) | collective-permute-done | bytes 196640 | tf_op jit(solution)/shard_map/ppermute | solution.py:325
  61.0 18.3 %weights.1 = (f32[32,64]{1,0:T(8,128)}, f32[64,512]{1,0:T(8,128)S(1)}, f32[384,512]{1,0:T(8,128)S(1)}) custom-call(f32[64,16,128]{2,1,0:T(8,128)S(1)} %all-to-all-done.mine_ref, f32[64,16,128]{2,1,0:T(8,128)S(1)} %collective-permute-done.2.other_ref, f32[2,64,384]{2,1,0:T(8,128)S(1)} %pad_maximum_fusion.2.p0_ref, ...), custom_call_target="tpu_custom_call" | custom-call | flops 30000001024 | bytes 1000000 | tf_op jit(solution)/shard_map/weights/pallas_call | solution.py:210
  79.3 0.0 collective-permute-done.12
  79.3 0.1 pad_maximum_fusion.refs_6_
  79.3 0.0 collective-permute-done.11.refs_5_
  79.3 0.0 collective-permute-done.10.refs_4_
  79.3 2.1 %collective-permute-start.13 = (f32[384,512]{1,0:T(8,128)S(1)}, f32[384,512]{1,0:T(8,128)S(1)}, u32[]{:S(2)}, u32[]{:S(2)}) collective-permute-start(f32[384,512]{1,0:T(8,128)S(1)} %get-tuple-element.47.mine_ref), channel_id=1, source_target_pairs={{0,8},{8,0},{1,9},{9,1},{2,10},{10,2},{3,11},{11,3},{4,12},{12,4},... | collective-permute-start | bytes 2359304 | tf_op jit(solution)/shard_map/ppermute | solution.py:325
  81.5 1.3 %collective-permute-start.14 = (f32[64,1024]{1,0:T(8,128)S(1)}, f32[64,1024]{1,0:T(8,128)S(1)}, u32[]{:S(2)}, u32[]{:S(2)}) collective-permute-start(f32[64,1024]{1,0:T(8,128)S(1)} %slice.29), channel_id=1, source_target_pairs={{0,1},{1,0},{2,3},{3,2},{4,5},{5,4},{6,7},{7,6},{8,9},{9,8},{10,11... | collective-permute-start | bytes 786440 | tf_op jit(solution)/shard_map/ppermute | solution.py:325
  82.8 0.0 collective-permute-start.15
  82.8 2.7 %collective-permute-start.16 = (f32[64,1024]{1,0:T(8,128)S(1)}, f32[64,1024]{1,0:T(8,128)S(1)}, u32[]{:S(2)}, u32[]{:S(2)}) collective-permute-start(f32[64,1024]{1,0:T(8,128)S(1)} %slice.31), channel_id=1, source_target_pairs={{0,6},{2,0},{4,2},{6,4},{1,7},{3,1},{5,3},{7,5},{8,14},{10,8},{12,... | collective-permute-start | bytes 786440 | tf_op jit(solution)/shard_map/ppermute | solution.py:325
  85.5 0.0 collective-permute-done.13.other_ref
  85.5 13.3 %update_start.1 = (f32[64,3072]{1,0:T(8,128)S(1)}, f32[3072,768]{1,0:T(8,128)S(1)}, bf16[512,768]{1,0:T(8,128)(2,1)S(1)}, bf16[512,768]{1,0:T(8,128)(2,1)S(1)}) custom-call(f32[384,512]{1,0:T(8,128)S(1)} %get-tuple-element.47.mine_ref, f32[384,512]{1,0:T(8,128)S(1)} %collective-permute-done.13.other_ref, f32[64,512]{1,0:T(8,128)S(1)} %get-tuple-element.42.own_ref, ...), custom_call_target="tpu_custom_call" | custom-call | flops 8000000000 | bytes 10000000 | tf_op jit(solution)/shard_map/update_start/pallas_call | solution.py:281
  98.8 0.0 collective-permute-done.14
  98.9 0.0 collective-permute-done.15
  98.9 0.1 pad_maximum_fusion.1.refs_0_
  98.9 5.8 %update_last.1 = (f32[64,3072]{1,0:T(8,128)}, f32[3072,768]{1,0:T(8,128)}) custom-call(f32[64,512]{1,0:T(8,128)S(1)} %get-tuple-element.42.own_ref, bf16[512,768]{1,0:T(8,128)(2,1)S(1)} %get-tuple-element.52.high_ref, bf16[512,768]{1,0:T(8,128)(2,1)S(1)} %get-tuple-element.53.low_ref, f32[64,3072]{1,0:T(8,128)S(1)} %pad_maximum_fusion.1.refs_0_, ...), custom_call_target="tpu_custom_call" | custom-call | flops 1000000000 | bytes 10000000 | tf_op jit(solution)/shard_map/update_last/pallas_call | solution.py:303
  (12 shorter events, 0.1 us)
Async XLA Ops:
  1.5 12.0 %collective-permute-start.1 = (f32[64,384]{1,0:T(8,128)S(1)}, f32[64,384]{1,0:T(8,128)S(1)}, u32[]{:S(2)}, u32[]{:S(2)}) collective-permute-start(f32[64,384]{1,0:T(8,128)S(1)} %slice.32), channel_id=1, source_target_pairs={{0,16},{1,0},{2,48},{3,32},{4,80},{5,64},{6,112},{7,96},{8,17},{9,... | collective-permute-start | bytes 294920 | tf_op jit(solution)/shard_map/ppermute | solution.py:354
  6.7 7.5 %collective-permute-start = (f32[64,384]{1,0:T(8,128)S(1)}, f32[64,384]{1,0:T(8,128)S(1)}, u32[]{:S(2)}, u32[]{:S(2)}) collective-permute-start(f32[64,384]{1,0:T(8,128)S(1)} %slice.32), channel_id=1, source_target_pairs={{0,0},{1,16},{2,32},{3,48},{4,64},{5,80},{6,96},{7,112},{8,1},{9,1... | collective-permute-start | bytes 294920 | tf_op jit(solution)/shard_map/ppermute | solution.py:354
  8.6 36.1 %collective-permute-start.5 = (f32[64,3072]{1,0:T(8,128)}, f32[64,3072]{1,0:T(8,128)S(1)}, u32[]{:S(2)}, u32[]{:S(2)}) collective-permute-start(f32[64,3072]{1,0:T(8,128)} %bitcast.5), channel_id=1, source_target_pairs={{0,6},{2,0},{4,2},{6,4},{1,7},{3,1},{5,3},{7,5},{8,14},{10,8},{12,... | collective-permute-start | bytes 2359304 | tf_op jit(solution)/shard_map/ppermute | solution.py:325
  15.8 26.0 %all-to-all-start = ((f32[64,16,128]{2,1,0:T(8,128)}), f32[64,16,128]{2,1,0:T(8,128)S(1)}, u32[]{:S(2)}, u32[]{:S(2)}) async-start(f32[64,16,128]{2,1,0:T(8,128)} %broadcast_in_dim.2), calls=%async_computation | async-start | bytes 1048576 | tf_op jit(solution)/shard_map/all_to_all | solution.py:335
  29.4 25.1 %collective-permute-start.4 = (f32[64,3072]{1,0:T(8,128)}, f32[64,3072]{1,0:T(8,128)S(1)}, u32[]{:S(2)}, u32[]{:S(2)}) collective-permute-start(f32[64,3072]{1,0:T(8,128)} %bitcast.6), channel_id=1, source_target_pairs={{0,2},{2,4},{4,6},{6,0},{1,3},{3,5},{5,7},{7,1},{8,10},{10,12},{12... | collective-permute-start | bytes 2359304 | tf_op jit(solution)/shard_map/ppermute | solution.py:325
  30.5 25.2 %collective-permute-start.3 = (f32[64,3072]{1,0:T(8,128)}, f32[64,3072]{1,0:T(8,128)S(1)}, u32[]{:S(2)}, u32[]{:S(2)}) collective-permute-start(f32[64,3072]{1,0:T(8,128)} %bitcast.7), channel_id=1, source_target_pairs={{0,1},{1,0},{2,3},{3,2},{4,5},{5,4},{6,7},{7,6},{8,9},{9,8},{10,11... | collective-permute-start | bytes 2359304 | tf_op jit(solution)/shard_map/ppermute | solution.py:325
  41.8 13.9 %collective-permute-start.2 = (f32[64,16,128]{2,1,0:T(8,128)S(1)}, f32[64,16,128]{2,1,0:T(8,128)S(1)}, u32[]{:S(2)}, u32[]{:S(2)}) collective-permute-start(f32[64,16,128]{2,1,0:T(8,128)S(1)} %all-to-all-done.mine_ref), channel_id=1, source_target_pairs={{0,8},{8,0},{1,9},{9,1},{2,10},{10,2},{3,11},{11,3},{4,12},{12,4},... | collective-permute-start | bytes 1572872 | tf_op jit(solution)/shard_map/ppermute | solution.py:325
  44.7 3.1 %collective-permute-start.6 = (f32[64,128]{1,0:T(8,128)S(1)}, f32[64,128]{1,0:T(8,128)S(1)}, u32[]{:S(2)}, u32[]{:S(2)}) collective-permute-start(f32[64,128]{1,0:T(8,128)S(1)} %slice.33), channel_id=1, source_target_pairs={{0,6},{2,0},{4,2},{6,4},{1,7},{3,1},{5,3},{7,5},{8,14},{10,8},{12,... | collective-permute-start | bytes 98312 | tf_op jit(solution)/shard_map/ppermute | solution.py:325
  47.8 9.9 %collective-permute-start.9 = (f32[2,64,384]{2,1,0:T(8,128)S(1)}, f32[2,64,384]{2,1,0:T(8,128)S(1)}, u32[]{:S(2)}, u32[]{:S(2)}) collective-permute-start(f32[2,64,384]{2,1,0:T(8,128)S(1)} %pad_maximum_fusion.2.p0_ref), channel_id=1, source_target_pairs={{0,96},{32,0},{64,32},{96,64},{1,97},{33,1},{65,33},{97,65},{2,98}... | collective-permute-start | bytes 589832 | tf_op jit(solution)/shard_map/ppermute | solution.py:325
  48.8 9.7 %collective-permute-start.8 = (f32[2,64,384]{2,1,0:T(8,128)S(1)}, f32[2,64,384]{2,1,0:T(8,128)S(1)}, u32[]{:S(2)}, u32[]{:S(2)}) collective-permute-start(f32[2,64,384]{2,1,0:T(8,128)S(1)} %pad_maximum_fusion.2.p0_ref), channel_id=1, source_target_pairs={{0,64},{32,96},{64,0},{96,32},{1,65},{33,97},{65,1},{97,33},{2,66}... | collective-permute-start | bytes 589832 | tf_op jit(solution)/shard_map/ppermute | solution.py:325
  54.5 6.5 %collective-permute-start.7 = (f32[2,64,384]{2,1,0:T(8,128)S(1)}, f32[2,64,384]{2,1,0:T(8,128)S(1)}, u32[]{:S(2)}, u32[]{:S(2)}) collective-permute-start(f32[2,64,384]{2,1,0:T(8,128)S(1)} %pad_maximum_fusion.2.p0_ref), channel_id=1, source_target_pairs={{0,32},{32,64},{64,96},{96,0},{1,33},{33,65},{65,97},{97,1},{2,34}... | collective-permute-start | bytes 589832 | tf_op jit(solution)/shard_map/ppermute | solution.py:325
  55.7 29.8 %slice-start = ((s8[9437184]{0:T(1024)(128)(4,1)}), s8[4194304]{0:T(1024)(128)(4,1)S(1)}, s32[]{:S(2)}) async-start(s8[9437184]{0:T(1024)(128)(4,1)} %bitcast.9), calls=%async_computation.1 | async-start | bytes 8388608
  55.8 29.7 %copy-start = (f32[3072,64]{0,1:T(8,128)S(1)}, f32[3072,64]{0,1:T(8,128)}, u32[]{:S(2)}) copy-start(f32[3072,64]{0,1:T(8,128)} %param.4) | copy-start | bytes 2359300
  55.8 29.7 %slice-start.1 = ((s8[9437184]{0:T(1024)(128)(4,1)}), s8[4194304]{0:T(1024)(128)(4,1)S(1)}, s32[]{:S(2)}) async-start(s8[9437184]{0:T(1024)(128)(4,1)} %bitcast.9), calls=%async_computation.2 | async-start | bytes 8388608
  55.8 29.7 %slice-start.2 = ((s8[9437184]{0:T(1024)(128)(4,1)}), s8[1048576]{0:T(1024)(128)(4,1)S(1)}, s32[]{:S(2)}) async-start(s8[9437184]{0:T(1024)(128)(4,1)} %bitcast.9), calls=%async_computation.3 | async-start | bytes 2097152
  55.8 23.5 %collective-permute-start.10 = (f32[64,3072]{1,0:T(8,128)S(1)}, f32[64,3072]{1,0:T(8,128)S(1)}, u32[]{:S(2)}, u32[]{:S(2)}) collective-permute-start(f32[64,3072]{1,0:T(8,128)S(1)} %collective-permute-done.5.refs_3_), channel_id=1, source_target_pairs={{0,1},{1,0},{2,3},{3,2},{4,5},{5,4},{6,7},{7,6},{8,9},{9,8},{10,11... | collective-permute-start | bytes 2359304 | tf_op jit(solution)/shard_map/ppermute | solution.py:325
  57.1 22.2 %collective-permute-start.12 = (f32[64,2944]{1,0:T(8,128)S(1)}, f32[64,2944]{1,0:T(8,128)S(1)}, u32[]{:S(2)}, u32[]{:S(2)}) collective-permute-start(f32[64,2944]{1,0:T(8,128)S(1)} %slice.28), channel_id=1, source_target_pairs={{0,6},{2,0},{4,2},{6,4},{1,7},{3,1},{5,3},{7,5},{8,14},{10,8},{12,... | collective-permute-start | bytes 2261000 | tf_op jit(solution)/shard_map/ppermute | solution.py:325
  57.7 21.6 %collective-permute-start.11 = (f32[64,3072]{1,0:T(8,128)S(1)}, f32[64,3072]{1,0:T(8,128)S(1)}, u32[]{:S(2)}, u32[]{:S(2)}) collective-permute-start(f32[64,3072]{1,0:T(8,128)S(1)} %collective-permute-done.3.refs_1_), channel_id=1, source_target_pairs={{0,2},{2,4},{4,6},{6,0},{1,3},{3,5},{5,7},{7,1},{8,10},{10,12},{12... | collective-permute-start | bytes 2359304 | tf_op jit(solution)/shard_map/ppermute | solution.py:325
  79.3 6.1 %collective-permute-start.13 = (f32[384,512]{1,0:T(8,128)S(1)}, f32[384,512]{1,0:T(8,128)S(1)}, u32[]{:S(2)}, u32[]{:S(2)}) collective-permute-start(f32[384,512]{1,0:T(8,128)S(1)} %get-tuple-element.47.mine_ref), channel_id=1, source_target_pairs={{0,8},{8,0},{1,9},{9,1},{2,10},{10,2},{3,11},{11,3},{4,12},{12,4},... | collective-permute-start | bytes 2359304 | tf_op jit(solution)/shard_map/ppermute | solution.py:325
  81.5 17.3 %collective-permute-start.14 = (f32[64,1024]{1,0:T(8,128)S(1)}, f32[64,1024]{1,0:T(8,128)S(1)}, u32[]{:S(2)}, u32[]{:S(2)}) collective-permute-start(f32[64,1024]{1,0:T(8,128)S(1)} %slice.29), channel_id=1, source_target_pairs={{0,1},{1,0},{2,3},{3,2},{4,5},{5,4},{6,7},{7,6},{8,9},{9,8},{10,11... | collective-permute-start | bytes 786440 | tf_op jit(solution)/shard_map/ppermute | solution.py:325
  82.8 16.1 %collective-permute-start.15 = (f32[64,1024]{1,0:T(8,128)S(1)}, f32[64,1024]{1,0:T(8,128)S(1)}, u32[]{:S(2)}, u32[]{:S(2)}) collective-permute-start(f32[64,1024]{1,0:T(8,128)S(1)} %slice.30), channel_id=1, source_target_pairs={{0,2},{2,4},{4,6},{6,0},{1,3},{3,5},{5,7},{7,1},{8,10},{10,12},{12... | collective-permute-start | bytes 786440 | tf_op jit(solution)/shard_map/ppermute | solution.py:325
  82.8 16.1 %collective-permute-start.16 = (f32[64,1024]{1,0:T(8,128)S(1)}, f32[64,1024]{1,0:T(8,128)S(1)}, u32[]{:S(2)}, u32[]{:S(2)}) collective-permute-start(f32[64,1024]{1,0:T(8,128)S(1)} %slice.31), channel_id=1, source_target_pairs={{0,6},{2,0},{4,2},{6,4},{1,7},{3,1},{5,3},{7,5},{8,14},{10,8},{12,... | collective-permute-start | bytes 786440 | tf_op jit(solution)/shard_map/ppermute | solution.py:325
where the time goes:
time: 105 us
  starting transfers between devices  45.2 us (43%)
  Pallas kernels  37.3 us (36%)
  waiting for transfers between devices  18.5 us (18%)
  local copies, waits for them, and re-layouts  2.59 us (2%)
    ppermute x15, starting transfers between devices, shift(): return lax.ppermute(x, axis, ring(lax.axis_size(axis), step))  24.5 us
    pallas_call x1, Pallas kernels, make_weights(): pl.pallas_call(weights_kernel, out_shape=[jax.ShapeDtypeStruct((WIDTH //...  18.3 us
    all_to_all x1, starting transfers between devices, gather_tiles(): lax.all_to_all(jnp.broadcast_to(flat[None], (64,) + flat.shape), ('y', 'z...  13.6 us
    pallas_call x1, Pallas kernels, update_start(): pl.pallas_call(start_kernel, grid=(rows // tile,), out_shape=[jax.ShapeDt...  13.3 us
    all_to_all x1, waiting for transfers between devices, gather_tiles(): lax.all_to_all(jnp.broadcast_to(flat[None], (64,) + flat.shape), ('y', 'z...  10.1 us
    ppermute x15, waiting for transfers between devices, shift(): return lax.ppermute(x, axis, ring(lax.axis_size(axis), step))  7.75 us
    ppermute x2, starting transfers between devices, shards(): pieces = [lax.ppermute(raw, everything, top_moves(flip)) for flip in (0, 1)]  7.06 us
    pallas_call x1, Pallas kernels, update_more(): pl.pallas_call(functools.partial(go_on_kernel, place=place), grid=(rows /...  5.76 us
  transfers between devices with their start and end apart: 18, of which 5 were waited for; matrix products, arithmetic and copies ran while one was open for 2% of the time, Pallas kernels for 30%

commit v1 on v0

--- a/solution.py
+++ b/solution.py
@@ -161,6 +161,18 @@
             r_ref[e:, o:e] = -z[:, o:]
 
 
+def first_half_kernel(mine_ref, other_ref, r_ref, u_ref, m_ref, t_ref, wide_ref, tall_ref):
+    assemble(mine_ref, other_ref, wide_ref, tall_ref, r_ref)
+    u_ref[...] = jnp.zeros_like(u_ref)
+    m_ref[...] = jnp.zeros_like(m_ref)
+    factor_steps((0, BLK), r_ref, u_ref, m_ref, t_ref)
+
+
+def second_half_kernel(r_in, u_in, m_in, r_ref, u_ref, m_ref, t_ref):
+    del r_in, u_in, m_in
+    factor_steps((2 * BLK, 3 * BLK), r_ref, u_ref, m_ref, t_ref)
+
+
 VMEM = pl.BlockSpec(memory_space=pltpu.VMEM)
 
 
@@ -168,17 +180,44 @@
     return pl.CostEstimate(flops=flops, bytes_accessed=bytes_accessed, transcendentals=0)
 
 
+SQUARES = [jax.ShapeDtypeStruct((WIDTH, WIDTH), jnp.float32)] * 3
+
+
+def factor_first(mine, other):
+    return pl.pallas_call(
+        first_half_kernel,
+        out_shape=SQUARES,
+        in_specs=[VMEM] * 2,
+        out_specs=[VMEM] * 3,
+        scratch_shapes=[
+            pltpu.VMEM((BLK, BLK), jnp.float32),
+            pltpu.VMEM((4 * WIDTH, BLK), jnp.float32),
+            pltpu.VMEM((4 * WIDTH, BLK), jnp.float32),
+        ],
+        cost_estimate=cost(10**6, 10**3),
+        compiler_params=pltpu.CompilerParams(vmem_limit_bytes=16 << 20),
+        name="factor_first",
+    )(mine, other)
+
+
+def factor_second(state):
+    return pl.pallas_call(
+        second_half_kernel,
+        out_shape=SQUARES,
+        in_specs=[VMEM] * 3,
+        out_specs=[VMEM] * 3,
+        input_output_aliases={0: 0, 1: 1, 2: 2},
+        scratch_shapes=[pltpu.VMEM((BLK, BLK), jnp.float32)],
+        cost_estimate=cost(3 * 10**10, 10**6),
+        compiler_params=pltpu.CompilerParams(vmem_limit_bytes=16 << 20),
+        name="factor_second",
+    )(*state)
+
+
 PLACES = ((0, 0), (0, 1), (3, 0), (1, 0), (1, 1), (3, 1), (2, 0), (2, 1))
 
 
-def weights_kernel(
-    mine_ref, other_ref, p0_ref, p1_ref, p2_ref, p3_ref, d_ref, own_ref, w_ref,
-    r_ref, u_ref, m_ref, b_ref, wide_ref, t_ref, k_ref, p_ref,
-):
-    assemble(mine_ref, other_ref, wide_ref, t_ref, r_ref)
-    u_ref[...] = jnp.zeros_like(u_ref)
-    m_ref[...] = jnp.zeros_like(m_ref)
-    factor_steps(range(0, WIDTH, BLK), r_ref, u_ref, m_ref, b_ref)
+def weights_kernel(u_ref, m_ref, p0_ref, p1_ref, p2_ref, p3_ref, d_ref, own_ref, w_ref, t_ref, k_ref, p_ref):
     y, zh, core = lax.axis_index("y"), lax.axis_index("zh"), lax.axis_index("core")
     x, zl = lax.axis_index("x"), lax.axis_index("zl")
     col, row = x * 2 + zl, (y * 2 + zh) * 2 + core
@@ -205,8 +244,7 @@
     d_ref[...] = t_ref[pl.ds(row, WIDTH // 16, stride=16), :][:, half:]
 
 
-def make_weights(mine, other, pairs):
-    square, tall = pltpu.VMEM((WIDTH, WIDTH), jnp.float32), pltpu.VMEM((4 * WIDTH, BLK), jnp.float32)
+def make_weights(upper, inverse, pairs):
     return pl.pallas_call(
         weights_kernel,
         out_shape=[
@@ -216,12 +254,12 @@
         ],
         in_specs=[VMEM] * 6,
         out_specs=[VMEM] * 3,
-        scratch_shapes=[square] * 3
-        + [pltpu.VMEM((BLK, BLK), jnp.float32), tall, tall, square, square],
-        cost_estimate=cost(3 * 10**10, 10**6),
+        scratch_shapes=[pltpu.VMEM((4 * WIDTH, BLK), jnp.float32)]
+        + [pltpu.VMEM((WIDTH, WIDTH), jnp.float32)] * 2,
+        cost_estimate=cost(10**6, 10**3),
         compiler_params=pltpu.CompilerParams(vmem_limit_bytes=24 << 20),
         name="weights",
-    )(mine, other, *pairs)
+    )(upper, inverse, *pairs)
 
 
 def split(a):
@@ -274,7 +312,7 @@
     return pl.BlockSpec(shape, lambda i: (0, 0))
 
 
-def update_start(mine, other, own, blocks, trailing, tile=256):
+def update_start(mine, other, own, blocks, trailing, tile=512):
     rows, columns = trailing.shape
     lanes = pl.BlockSpec((WIDTH // 8, tile), lambda i: (0, i))
     wide = pl.BlockSpec((tile, columns), lambda i: (i, 0))
@@ -291,7 +329,7 @@
         out_specs=[lanes, wide] + [whole((WIDTH, columns))] * 2,
         scratch_shapes=[pltpu.VMEM((columns * WIDTH // BLK, BLK), jnp.float32)],
         cost_estimate=cost(8 * 10**9, 10**7),
-        compiler_params=pltpu.CompilerParams(vmem_limit_bytes=20 << 20),
+        compiler_params=pltpu.CompilerParams(vmem_limit_bytes=24 << 20),
         name="update_start",
     )(mine, other, own, *blocks, trailing)
 
@@ -312,7 +350,7 @@
         + [wide],
         out_specs=[lanes, wide],
         cost_estimate=cost(10**9 * len(blocks), 10**7),
-        compiler_params=pltpu.CompilerParams(vmem_limit_bytes=16 << 20),
+        compiler_params=pltpu.CompilerParams(vmem_limit_bytes=24 << 20),
         name=name,
     )(own, high, low, *blocks, pf, trailing)
 
@@ -349,39 +387,40 @@
 def shards(diag_block, panel_below, trailing):
     panel_t = panel_below.T
     top_len = trailing.shape[1] // 2
+    mine = gather_tiles(diag_block)
+    from_z = shift(panel_t, "zl", 1)
+    from_l = shift(panel_t, "x", 1)
+    from_r = shift(panel_t, "x", -1)
     everything = ("y", "zh", "core", "x", "zl")
     raw = panel_t[:, :top_len]
     pieces = [lax.ppermute(raw, everything, top_moves(flip)) for flip in (0, 1)]
-    diag_block, *pieces = order(diag_block, *pieces)
-    from_z = shift(panel_t, "zl", 1)
-    from_l = shift(panel_t, "x", 1)
-    from_r = shift(panel_t, "x", -1)
-    mine = gather_tiles(diag_block)
-    head = BLK
-    ahead = shift(from_r[:, :head], "x", -1)
-    ahead, *pieces = order(ahead, *pieces)
+    other = shift(mine, "core", 1)
+    state = factor_first(mine, other)
+    *state, from_z, from_l, from_r = order(*state, from_z, from_l, from_r)
+    from_rz = shift(from_r, "zl", 1)
+    from_lz = shift(from_z, "x", 1)
+    from_2 = shift(from_r, "x", -1)
+    _, upper, inverse = factor_second(state)
+    upper, inverse, *pieces = order(upper, inverse, *pieces)
     pair = jnp.stack(pieces)
     pairs = [pair] + [shift(pair, "y", s) for s in (1, 2, 3)]
-    other = shift(mine, "core", 1)
-    mine, other, from_z, from_l, from_r, ahead = order(mine, other, from_z, from_l, from_r, ahead)
-    from_rz = shift(from_r, "zl", 1)
-    from_lz = shift(from_z, "x", 1)
-    from_2 = jnp.concatenate([ahead, shift(from_r[:, head:], "x", -1)], axis=1)
-    diag_factor, own, weights = make_weights(mine, other, pairs)
-    weights, from_rz, from_lz, from_2 = order(weights, from_rz, from_lz, from_2)
-    weights_other = shift(weights, "core", 1)
+    upper, inverse, from_rz, from_lz, from_2, *pairs = order(
+        upper, inverse, from_rz, from_lz, from_2, *pairs
+    )
+    diag_factor, own, weights = make_weights(upper, inverse, pairs)
     third = panel_t.shape[1] // 3
     parts = (
         shift(from_2[:, :third], "zl", 1),
         shift(from_lz[:, third : 2 * third], "x", 1),
         shift(from_rz[:, 2 * third :], "x", -1),
     )
+    weights_other = shift(weights, "core", 1)
     blocks = [panel_t, from_z, from_l, from_r, from_rz, from_lz, from_2]
     factor_part, rest, high, low = update_start(weights, weights_other, own, blocks, trailing)
     factor_part, rest, *parts = order(factor_part, rest, *parts)
     from_2z = jnp.concatenate(parts, axis=1)
     panel_factor, new_trailing = update_more(
-        7, own, high, low, [from_2z], factor_part, rest, 512, "update_last"
+        7, own, high, low, [from_2z], factor_part, rest, 1024, "update_last"
     )
     return (diag_factor, panel_factor.T, new_trailing)
 

time: 105 us -> 95 us (0.905)
  starting transfers between devices: 45.2 us -> 34.7 us
  waiting for transfers between devices: 18.5 us -> 21.3 us
  Pallas kernels: 37.3 us -> 35.1 us
    pallas_call x0 -> x2, Pallas kernels: none -> 14.4 us  [the longest x1 7.98 us: factor_first(): pl.pallas_call(first_half_kernel, out_shape=SQUARES, in_specs=[VMEM] * 2,...]
    pallas_call x1, Pallas kernels: 18.3 us -> 4.07 us  [make_weights(): pl.pallas_call(weights_kernel, out_shape=[jax.ShapeDtypeStruct((WIDTH //...]
    ppermute x15 -> x14, waiting for transfers between devices: 7.75 us -> 12.8 us  [shift(): return lax.ppermute(x, axis, ring(lax.axis_size(axis), step))]
    ppermute x15 -> x14, starting transfers between devices: 24.5 us -> 19.9 us  [shift(): return lax.ppermute(x, axis, ring(lax.axis_size(axis), step))]
    ppermute x2, starting transfers between devices: 7.06 us -> 2.9 us  [shards(): pieces = [lax.ppermute(raw, everything, top_moves(flip)) for flip in (0, 1)]]
    pallas_call x1, Pallas kernels: 13.3 us -> 11.6 us  [update_start(): pl.pallas_call(start_kernel, grid=(rows // tile,), out_shape=[jax.ShapeDt...]
    all_to_all x1, starting transfers between devices: 13.6 us -> 12 us  [gather_tiles(): lax.all_to_all(jnp.broadcast_to(flat[None], (64,) + flat.shape), ('y', 'z...]
    all_to_all x1, waiting for transfers between devices: 10.1 us -> 8.5 us  [gather_tiles(): lax.all_to_all(jnp.broadcast_to(flat[None], (64,) + flat.shape), ('y', 'z...]
  transfers between devices with their start and end apart: 18 -> 17, of which waited for: 5 -> 6; matrix products, arithmetic and copies ran while one was open for 2% -> 1% of each run, Pallas kernels for 30% -> 27%
where the time goes in v1:
time: 95 us; the launch traced here: 94.7 us
  Pallas kernels  35.1 us (37%)
  starting transfers between devices  34.7 us (37%)
  waiting for transfers between devices  21.3 us (22%)
  local copies, waits for them, and re-layouts  2.53 us (3%)
    ppermute x14, starting transfers between devices, shift(): return lax.ppermute(x, axis, ring(lax.axis_size(axis), step))  19.9 us
    ppermute x14, waiting for transfers between devices, shift(): return lax.ppermute(x, axis, ring(lax.axis_size(axis), step))  12.8 us
    all_to_all x1, starting transfers between devices, gather_tiles(): lax.all_to_all(jnp.broadcast_to(flat[None], (64,) + flat.shape), ('y', 'z...  12 us
    pallas_call x1, Pallas kernels, update_start(): pl.pallas_call(start_kernel, grid=(rows // tile,), out_shape=[jax.ShapeDt...  11.6 us
    all_to_all x1, waiting for transfers between devices, gather_tiles(): lax.all_to_all(jnp.broadcast_to(flat[None], (64,) + flat.shape), ('y', 'z...  8.5 us
    pallas_call x1, Pallas kernels, factor_first(): pl.pallas_call(first_half_kernel, out_shape=SQUARES, in_specs=[VMEM] * 2,...  7.98 us
    pallas_call x1, Pallas kernels, factor_second(): pl.pallas_call(second_half_kernel, out_shape=SQUARES, in_specs=[VMEM] * 3...  6.44 us
    pallas_call x1, Pallas kernels, update_more(): pl.pallas_call(functools.partial(go_on_kernel, place=place), grid=(rows /...  5.04 us
  transfers between devices with their start and end apart: 17, of which 6 were waited for; matrix products, arithmetic and copies ran while one was open for 1% of the time, Pallas kernels for 27%

profile of v1, /device:TPU:1, one launch (start us, length us, event | category | flops | bytes accessed | tf_op | source)
XLA Modules:
  0.0 94.7 jit_solution(5934591659797852532)
XLA Ops:
  0.6 0.7 fusion
  1.3 0.1 pad_maximum_fusion.2
  1.4 0.8 broadcast_in_dim.2
  2.3 12.0 %all-to-all-start = ((f32[64,16,128]{2,1,0:T(8,128)}), f32[64,16,128]{2,1,0:T(8,128)S(1)}, u32[]{:S(2)}, u32[]{:S(2)}) async-start(f32[64,16,128]{2,1,0:T(8,128)} %broadcast_in_dim.2), calls=%async_computation | async-start | bytes 1048576 | tf_op jit(solution)/shard_map/all_to_all | solution.py:373
  14.2 2.3 %collective-permute-start.3 = (f32[64,3072]{1,0:T(8,128)}, f32[64,3072]{1,0:T(8,128)S(1)}, u32[]{:S(2)}, u32[]{:S(2)}) collective-permute-start(f32[64,3072]{1,0:T(8,128)} %bitcast.4), channel_id=1, source_target_pairs={{0,6},{2,0},{4,2},{6,4},{1,7},{3,1},{5,3},{7,5},{8,14},{10,8},{12,... | collective-permute-start | bytes 2359304 | tf_op jit(solution)/shard_map/ppermute | solution.py:363
  16.5 0.0 collective-permute-start.2
  16.5 1.2 %collective-permute-start.1 = (f32[64,3072]{1,0:T(8,128)}, f32[64,3072]{1,0:T(8,128)S(1)}, u32[]{:S(2)}, u32[]{:S(2)}) collective-permute-start(f32[64,3072]{1,0:T(8,128)} %bitcast.6), channel_id=1, source_target_pairs={{0,1},{1,0},{2,3},{3,2},{4,5},{5,4},{6,7},{7,6},{8,9},{9,8},{10,11... | collective-permute-start | bytes 2359304 | tf_op jit(solution)/shard_map/ppermute | solution.py:363
  17.7 8.5 %all-to-all-done.mine_ref = f32[64,16,128]{2,1,0:T(8,128)S(1)} async-done(((f32[64,16,128]{2,1,0:T(8,128)}), f32[64,16,128]{2,1,0:T(8,128)S(1)}, u32[]{:S(2)}, u32[]{:S(2)}) %all-to-all-start) | async-done | bytes 524320 | tf_op jit(solution)/shard_map/all_to_all | solution.py:373
  26.2 3.6 %collective-permute-start = (f32[64,16,128]{2,1,0:T(8,128)S(1)}, f32[64,16,128]{2,1,0:T(8,128)S(1)}, u32[]{:S(2)}, u32[]{:S(2)}) collective-permute-start(f32[64,16,128]{2,1,0:T(8,128)S(1)} %all-to-all-done.mine_ref), channel_id=1, source_target_pairs={{0,8},{8,0},{1,9},{9,1},{2,10},{10,2},{3,11},{11,3},{4,12},{12,4},... | collective-permute-start | bytes 1572872 | tf_op jit(solution)/shard_map/ppermute | solution.py:363
  29.8 0.9 slice.24
  30.7 0.0 collective-permute-start.5
  30.7 0.6 collective-permute-done.other_ref
  31.4 2.9 %collective-permute-start.4 = (f32[64,384]{1,0:T(8,128)S(1)}, f32[64,384]{1,0:T(8,128)S(1)}, u32[]{:S(2)}, u32[]{:S(2)}) collective-permute-start(f32[64,384]{1,0:T(8,128)S(1)} %slice.24), channel_id=1, source_target_pairs={{0,0},{1,16},{2,32},{3,48},{4,64},{5,80},{6,96},{7,112},{8,1},{9,1... | collective-permute-start | bytes 294920 | tf_op jit(solution)/shard_map/ppermute | solution.py:396
  34.3 8.0 %factor_first.1 = (f32[512,512]{1,0:T(8,128)S(1)}, f32[512,512]{1,0:T(8,128)S(1)}, f32[512,512]{1,0:T(8,128)S(1)}) custom-call(f32[64,16,128]{2,1,0:T(8,128)S(1)} %all-to-all-done.mine_ref, f32[64,16,128]{2,1,0:T(8,128)S(1)} %collective-permute-done.other_ref), custom_call_target="tpu_custom_call" | custom-call | flops 1000000 | bytes 1000 | tf_op jit(solution)/shard_map/factor_first/pallas_call | solution.py:187
  42.3 0.0 collective-permute-done.3.refs_3_
  42.3 0.0 collective-permute-done.2.refs_2_
  42.3 0.0 collective-permute-done.1.refs_1_
  42.3 0.0 slice-start
  42.3 0.0 copy-start
  42.3 0.0 slice-start.1
  42.3 0.0 slice-start.2
  42.3 5.5 %collective-permute-start.8 = (f32[64,3072]{1,0:T(8,128)S(1)}, f32[64,3072]{1,0:T(8,128)S(1)}, u32[]{:S(2)}, u32[]{:S(2)}) collective-permute-start(f32[64,3072]{1,0:T(8,128)S(1)} %collective-permute-done.3.refs_3_), channel_id=1, source_target_pairs={{0,6},{2,0},{4,2},{6,4},{1,7},{3,1},{5,3},{7,5},{8,14},{10,8},{12,... | collective-permute-start | bytes 2359304 | tf_op jit(solution)/shard_map/ppermute | solution.py:363
  47.8 0.5 collective-permute-start.6
  48.4 0.0 collective-permute-start.7
  48.4 6.4 %factor_second.1 = (f32[512,512]{1,0:T(8,128)S(1)}, f32[512,512]{1,0:T(8,128)S(1)}, f32[512,512]{1,0:T(8,128)S(1)}) custom-call(f32[512,512]{1,0:T(8,128)S(1)} %get-tuple-element.44.r_in, f32[512,512]{1,0:T(8,128)S(1)} %get-tuple-element.45.u_in, f32[512,512]{1,0:T(8,128)S(1)} %get-tuple-element.46.m_in), custom_call_target="tpu_custom_call", output_to_operand_aliasing={{0}: (0, {}), {1}: (1, {}), {2}: (2, {})} | custom-call | flops 30000001024 | bytes 1000000 | tf_op jit(solution)/shard_map/factor_second/pallas_call | solution.py:204
  54.8 0.0 collective-permute-done.5
  54.9 0.0 collective-permute-done.4
  54.9 0.4 collective-permute-start.11
  55.3 1.4 %collective-permute-start.10 = (f32[2,64,384]{2,1,0:T(8,128)S(1)}, f32[2,64,384]{2,1,0:T(8,128)S(1)}, u32[]{:S(2)}, u32[]{:S(2)}) collective-permute-start(f32[2,64,384]{2,1,0:T(8,128)S(1)} %pad_maximum_fusion.1.p0_ref), channel_id=1, source_target_pairs={{0,64},{32,96},{64,0},{96,32},{1,65},{33,97},{65,1},{97,33},{2,66}... | collective-permute-start | bytes 589832 | tf_op jit(solution)/shard_map/ppermute | solution.py:363
  56.7 4.7 %collective-permute-done.11.p3_ref = f32[2,64,384]{2,1,0:T(8,128)S(1)} collective-permute-done((f32[2,64,384]{2,1,0:T(8,128)S(1)}, f32[2,64,384]{2,1,0:T(8,128)S(1)}, u32[]{:S(2)}, u32[]{:S(2)}) %collective-permute-start.11) | collective-permute-done | bytes 196640 | tf_op jit(solution)/shard_map/ppermute | solution.py:363
  61.4 0.0 collective-permute-start.9
  61.4 1.2 %collective-permute-done.10.p2_ref = f32[2,64,384]{2,1,0:T(8,128)S(1)} collective-permute-done((f32[2,64,384]{2,1,0:T(8,128)S(1)}, f32[2,64,384]{2,1,0:T(8,128)S(1)}, u32[]{:S(2)}, u32[]{:S(2)}) %collective-permute-start.10) | collective-permute-done | bytes 196640 | tf_op jit(solution)/shard_map/ppermute | solution.py:363
  62.6 5.0 %collective-permute-done.9.p1_ref = f32[2,64,384]{2,1,0:T(8,128)S(1)} collective-permute-done((f32[2,64,384]{2,1,0:T(8,128)S(1)}, f32[2,64,384]{2,1,0:T(8,128)S(1)}, u32[]{:S(2)}, u32[]{:S(2)}) %collective-permute-start.9) | collective-permute-done | bytes 196640 | tf_op jit(solution)/shard_map/ppermute | solution.py:363
  67.7 1.2 %collective-permute-done.7.refs_5_ = f32[64,3072]{1,0:T(8,128)S(1)} collective-permute-done((f32[64,3072]{1,0:T(8,128)S(1)}, f32[64,3072]{1,0:T(8,128)S(1)}, u32[]{:S(2)}, u32[]{:S(2)}) %collective-permute-start.7) | collective-permute-done | bytes 786464 | tf_op jit(solution)/shard_map/ppermute | solution.py:363
  68.8 0.0 collective-permute-done.8.refs_6_
  68.8 0.0 collective-permute-done.6.refs_4_
  68.9 4.1 %weights.1 = (f32[32,64]{1,0:T(8,128)}, f32[64,512]{1,0:T(8,128)S(1)}, f32[384,512]{1,0:T(8,128)S(1)}) custom-call(f32[512,512]{1,0:T(8,128)S(1)} %get-tuple-element.55.u_ref, f32[512,512]{1,0:T(8,128)S(1)} %get-tuple-element.56.m_ref, f32[2,64,384]{2,1,0:T(8,128)S(1)} %pad_maximum_fusion.1.p0_ref, f32[2,64,384]{2,1,0:T(8,128)S(1)} %collective-permute-done.9.p1_ref, ...), custom_call_target="tpu_custom_call" | custom-call | flops 1000000 | bytes 1000 | tf_op jit(solution)/shard_map/weights/pallas_call | solution.py:248
  72.9 1.1 %collective-permute-start.12 = (f32[384,512]{1,0:T(8,128)S(1)}, f32[384,512]{1,0:T(8,128)S(1)}, u32[]{:S(2)}, u32[]{:S(2)}) collective-permute-start(f32[384,512]{1,0:T(8,128)S(1)} %get-tuple-element.63.mine_ref), channel_id=1, source_target_pairs={{0,8},{8,0},{1,9},{9,1},{2,10},{10,2},{3,11},{11,3},{4,12},{12,4},... | collective-permute-start | bytes 2359304 | tf_op jit(solution)/shard_map/ppermute | solution.py:363
  74.1 1.1 %collective-permute-start.13 = (f32[64,1024]{1,0:T(8,128)S(1)}, f32[64,1024]{1,0:T(8,128)S(1)}, u32[]{:S(2)}, u32[]{:S(2)}) collective-permute-start(f32[64,1024]{1,0:T(8,128)S(1)} %slice.21), channel_id=1, source_target_pairs={{0,1},{1,0},{2,3},{3,2},{4,5},{5,4},{6,7},{7,6},{8,9},{9,8},{10,11... | collective-permute-start | bytes 786440 | tf_op jit(solution)/shard_map/ppermute | solution.py:363
  75.2 0.6 collective-permute-start.14
  75.9 2.0 %collective-permute-start.15 = (f32[64,1024]{1,0:T(8,128)S(1)}, f32[64,1024]{1,0:T(8,128)S(1)}, u32[]{:S(2)}, u32[]{:S(2)}) collective-permute-start(f32[64,1024]{1,0:T(8,128)S(1)} %slice.23), channel_id=1, source_target_pairs={{0,6},{2,0},{4,2},{6,4},{1,7},{3,1},{5,3},{7,5},{8,14},{10,8},{12,... | collective-permute-start | bytes 786440 | tf_op jit(solution)/shard_map/ppermute | solution.py:363
  77.9 0.0 collective-permute-done.12.other_ref
  78.0 11.6 %update_start.1 = (f32[64,3072]{1,0:T(8,128)S(1)}, f32[3072,768]{1,0:T(8,128)S(1)}, bf16[512,768]{1,0:T(8,128)(2,1)S(1)}, bf16[512,768]{1,0:T(8,128)(2,1)S(1)}) custom-call(f32[384,512]{1,0:T(8,128)S(1)} %get-tuple-element.63.mine_ref, f32[384,512]{1,0:T(8,128)S(1)} %collective-permute-done.12.other_ref, f32[64,512]{1,0:T(8,128)S(1)} %get-tuple-element.62.own_ref, ...), custom_call_target="tpu_custom_call" | custom-call | flops 8000000000 | bytes 10000000 | tf_op jit(solution)/shard_map/update_start/pallas_call | solution.py:319
  89.5 0.0 collective-permute-done.13
  89.5 0.0 collective-permute-done.14
  89.5 0.0 collective-permute-done.15
  89.5 0.1 pad_maximum_fusion.refs_0_
  89.6 5.0 %update_last.1 = (f32[64,3072]{1,0:T(8,128)}, f32[3072,768]{1,0:T(8,128)}) custom-call(f32[64,512]{1,0:T(8,128)S(1)} %get-tuple-element.62.own_ref, bf16[512,768]{1,0:T(8,128)(2,1)S(1)} %get-tuple-element.68.high_ref, bf16[512,768]{1,0:T(8,128)(2,1)S(1)} %get-tuple-element.69.low_ref, f32[64,3072]{1,0:T(8,128)S(1)} %pad_maximum_fusion.refs_0_, ...), custom_call_target="tpu_custom_call" | custom-call | flops 1000000000 | bytes 10000000 | tf_op jit(solution)/shard_map/update_last/pallas_call | solution.py:341
  (9 shorter events, 0.1 us)
Async XLA Ops:
  2.3 24.0 %all-to-all-start = ((f32[64,16,128]{2,1,0:T(8,128)}), f32[64,16,128]{2,1,0:T(8,128)S(1)}, u32[]{:S(2)}, u32[]{:S(2)}) async-start(f32[64,16,128]{2,1,0:T(8,128)} %broadcast_in_dim.2), calls=%async_computation | async-start | bytes 1048576 | tf_op jit(solution)/shard_map/all_to_all | solution.py:373
  14.2 28.0 %collective-permute-start.3 = (f32[64,3072]{1,0:T(8,128)}, f32[64,3072]{1,0:T(8,128)S(1)}, u32[]{:S(2)}, u32[]{:S(2)}) collective-permute-start(f32[64,3072]{1,0:T(8,128)} %bitcast.4), channel_id=1, source_target_pairs={{0,6},{2,0},{4,2},{6,4},{1,7},{3,1},{5,3},{7,5},{8,14},{10,8},{12,... | collective-permute-start | bytes 2359304 | tf_op jit(solution)/shard_map/ppermute | solution.py:363
  16.5 25.8 %collective-permute-start.2 = (f32[64,3072]{1,0:T(8,128)}, f32[64,3072]{1,0:T(8,128)S(1)}, u32[]{:S(2)}, u32[]{:S(2)}) collective-permute-start(f32[64,3072]{1,0:T(8,128)} %bitcast.5), channel_id=1, source_target_pairs={{0,2},{2,4},{4,6},{6,0},{1,3},{3,5},{5,7},{7,1},{8,10},{10,12},{12... | collective-permute-start | bytes 2359304 | tf_op jit(solution)/shard_map/ppermute | solution.py:363
  16.5 25.8 %collective-permute-start.1 = (f32[64,3072]{1,0:T(8,128)}, f32[64,3072]{1,0:T(8,128)S(1)}, u32[]{:S(2)}, u32[]{:S(2)}) collective-permute-start(f32[64,3072]{1,0:T(8,128)} %bitcast.6), channel_id=1, source_target_pairs={{0,1},{1,0},{2,3},{3,2},{4,5},{5,4},{6,7},{7,6},{8,9},{9,8},{10,11... | collective-permute-start | bytes 2359304 | tf_op jit(solution)/shard_map/ppermute | solution.py:363
  26.2 5.2 %collective-permute-start = (f32[64,16,128]{2,1,0:T(8,128)S(1)}, f32[64,16,128]{2,1,0:T(8,128)S(1)}, u32[]{:S(2)}, u32[]{:S(2)}) collective-permute-start(f32[64,16,128]{2,1,0:T(8,128)S(1)} %all-to-all-done.mine_ref), channel_id=1, source_target_pairs={{0,8},{8,0},{1,9},{9,1},{2,10},{10,2},{3,11},{11,3},{4,12},{12,4},... | collective-permute-start | bytes 1572872 | tf_op jit(solution)/shard_map/ppermute | solution.py:363
  30.7 24.1 %collective-permute-start.5 = (f32[64,384]{1,0:T(8,128)S(1)}, f32[64,384]{1,0:T(8,128)S(1)}, u32[]{:S(2)}, u32[]{:S(2)}) collective-permute-start(f32[64,384]{1,0:T(8,128)S(1)} %slice.24), channel_id=1, source_target_pairs={{0,16},{1,0},{2,48},{3,32},{4,80},{5,64},{6,112},{7,96},{8,17},{9,... | collective-permute-start | bytes 294920 | tf_op jit(solution)/shard_map/ppermute | solution.py:396
  31.4 23.5 %collective-permute-start.4 = (f32[64,384]{1,0:T(8,128)S(1)}, f32[64,384]{1,0:T(8,128)S(1)}, u32[]{:S(2)}, u32[]{:S(2)}) collective-permute-start(f32[64,384]{1,0:T(8,128)S(1)} %slice.24), channel_id=1, source_target_pairs={{0,0},{1,16},{2,32},{3,48},{4,64},{5,80},{6,96},{7,112},{8,1},{9,1... | collective-permute-start | bytes 294920 | tf_op jit(solution)/shard_map/ppermute | solution.py:396
  42.3 35.6 %slice-start = ((s8[9437184]{0:T(1024)(128)(4,1)}), s8[4194304]{0:T(1024)(128)(4,1)S(1)}, s32[]{:S(2)}) async-start(s8[9437184]{0:T(1024)(128)(4,1)} %bitcast.9), calls=%async_computation.1 | async-start | bytes 8388608
  42.3 35.6 %copy-start = (f32[3072,64]{0,1:T(8,128)S(1)}, f32[3072,64]{0,1:T(8,128)}, u32[]{:S(2)}) copy-start(f32[3072,64]{0,1:T(8,128)} %param.4) | copy-start | bytes 2359300
  42.3 35.6 %slice-start.1 = ((s8[9437184]{0:T(1024)(128)(4,1)}), s8[4194304]{0:T(1024)(128)(4,1)S(1)}, s32[]{:S(2)}) async-start(s8[9437184]{0:T(1024)(128)(4,1)} %bitcast.9), calls=%async_computation.2 | async-start | bytes 8388608
  42.3 35.6 %slice-start.2 = ((s8[9437184]{0:T(1024)(128)(4,1)}), s8[1048576]{0:T(1024)(128)(4,1)S(1)}, s32[]{:S(2)}) async-start(s8[9437184]{0:T(1024)(128)(4,1)} %bitcast.9), calls=%async_computation.3 | async-start | bytes 2097152
  42.3 26.5 %collective-permute-start.8 = (f32[64,3072]{1,0:T(8,128)S(1)}, f32[64,3072]{1,0:T(8,128)S(1)}, u32[]{:S(2)}, u32[]{:S(2)}) collective-permute-start(f32[64,3072]{1,0:T(8,128)S(1)} %collective-permute-done.3.refs_3_), channel_id=1, source_target_pairs={{0,6},{2,0},{4,2},{6,4},{1,7},{3,1},{5,3},{7,5},{8,14},{10,8},{12,... | collective-permute-start | bytes 2359304 | tf_op jit(solution)/shard_map/ppermute | solution.py:363
  47.8 21.0 %collective-permute-start.6 = (f32[64,3072]{1,0:T(8,128)S(1)}, f32[64,3072]{1,0:T(8,128)S(1)}, u32[]{:S(2)}, u32[]{:S(2)}) collective-permute-start(f32[64,3072]{1,0:T(8,128)S(1)} %collective-permute-done.3.refs_3_), channel_id=1, source_target_pairs={{0,1},{1,0},{2,3},{3,2},{4,5},{5,4},{6,7},{7,6},{8,9},{9,8},{10,11... | collective-permute-start | bytes 2359304 | tf_op jit(solution)/shard_map/ppermute | solution.py:363
  48.4 20.5 %collective-permute-start.7 = (f32[64,3072]{1,0:T(8,128)S(1)}, f32[64,3072]{1,0:T(8,128)S(1)}, u32[]{:S(2)}, u32[]{:S(2)}) collective-permute-start(f32[64,3072]{1,0:T(8,128)S(1)} %collective-permute-done.1.refs_1_), channel_id=1, source_target_pairs={{0,2},{2,4},{4,6},{6,0},{1,3},{3,5},{5,7},{7,1},{8,10},{10,12},{12... | collective-permute-start | bytes 2359304 | tf_op jit(solution)/shard_map/ppermute | solution.py:363
  54.9 6.5 %collective-permute-start.11 = (f32[2,64,384]{2,1,0:T(8,128)S(1)}, f32[2,64,384]{2,1,0:T(8,128)S(1)}, u32[]{:S(2)}, u32[]{:S(2)}) collective-permute-start(f32[2,64,384]{2,1,0:T(8,128)S(1)} %pad_maximum_fusion.1.p0_ref), channel_id=1, source_target_pairs={{0,96},{32,0},{64,32},{96,64},{1,97},{33,1},{65,33},{97,65},{2,98}... | collective-permute-start | bytes 589832 | tf_op jit(solution)/shard_map/ppermute | solution.py:363
  55.3 7.3 %collective-permute-start.10 = (f32[2,64,384]{2,1,0:T(8,128)S(1)}, f32[2,64,384]{2,1,0:T(8,128)S(1)}, u32[]{:S(2)}, u32[]{:S(2)}) collective-permute-start(f32[2,64,384]{2,1,0:T(8,128)S(1)} %pad_maximum_fusion.1.p0_ref), channel_id=1, source_target_pairs={{0,64},{32,96},{64,0},{96,32},{1,65},{33,97},{65,1},{97,33},{2,66}... | collective-permute-start | bytes 589832 | tf_op jit(solution)/shard_map/ppermute | solution.py:363
  61.4 6.3 %collective-permute-start.9 = (f32[2,64,384]{2,1,0:T(8,128)S(1)}, f32[2,64,384]{2,1,0:T(8,128)S(1)}, u32[]{:S(2)}, u32[]{:S(2)}) collective-permute-start(f32[2,64,384]{2,1,0:T(8,128)S(1)} %pad_maximum_fusion.1.p0_ref), channel_id=1, source_target_pairs={{0,32},{32,64},{64,96},{96,0},{1,33},{33,65},{65,97},{97,1},{2,34}... | collective-permute-start | bytes 589832 | tf_op jit(solution)/shard_map/ppermute | solution.py:363
  72.9 5.0 %collective-permute-start.12 = (f32[384,512]{1,0:T(8,128)S(1)}, f32[384,512]{1,0:T(8,128)S(1)}, u32[]{:S(2)}, u32[]{:S(2)}) collective-permute-start(f32[384,512]{1,0:T(8,128)S(1)} %get-tuple-element.63.mine_ref), channel_id=1, source_target_pairs={{0,8},{8,0},{1,9},{9,1},{2,10},{10,2},{3,11},{11,3},{4,12},{12,4},... | collective-permute-start | bytes 2359304 | tf_op jit(solution)/shard_map/ppermute | solution.py:363
  74.1 15.4 %collective-permute-start.13 = (f32[64,1024]{1,0:T(8,128)S(1)}, f32[64,1024]{1,0:T(8,128)S(1)}, u32[]{:S(2)}, u32[]{:S(2)}) collective-permute-start(f32[64,1024]{1,0:T(8,128)S(1)} %slice.21), channel_id=1, source_target_pairs={{0,1},{1,0},{2,3},{3,2},{4,5},{5,4},{6,7},{7,6},{8,9},{9,8},{10,11... | collective-permute-start | bytes 786440 | tf_op jit(solution)/shard_map/ppermute | solution.py:363
  75.2 14.3 %collective-permute-start.14 = (f32[64,1024]{1,0:T(8,128)S(1)}, f32[64,1024]{1,0:T(8,128)S(1)}, u32[]{:S(2)}, u32[]{:S(2)}) collective-permute-start(f32[64,1024]{1,0:T(8,128)S(1)} %slice.22), channel_id=1, source_target_pairs={{0,2},{2,4},{4,6},{6,0},{1,3},{3,5},{5,7},{7,1},{8,10},{10,12},{12... | collective-permute-start | bytes 786440 | tf_op jit(solution)/shard_map/ppermute | solution.py:363
  75.9 13.7 %collective-permute-start.15 = (f32[64,1024]{1,0:T(8,128)S(1)}, f32[64,1024]{1,0:T(8,128)S(1)}, u32[]{:S(2)}, u32[]{:S(2)}) collective-permute-start(f32[64,1024]{1,0:T(8,128)S(1)} %slice.23), channel_id=1, source_target_pairs={{0,6},{2,0},{4,2},{6,4},{1,7},{3,1},{5,3},{7,5},{8,14},{10,8},{12,... | collective-permute-start | bytes 786440 | tf_op jit(solution)/shard_map/ppermute | solution.py:363

commit v2 on v1

--- a/solution.py
+++ b/solution.py
@@ -232,8 +232,8 @@
     top = jnp.concatenate(
         [ref[i] for ref in (p0_ref, p1_ref, p2_ref, p3_ref) for i in range(2)], axis=0
     )
-    solved = dot(top, k_ref[...], 0, 0)
-    w_ref[...] = dot(solved, p_ref[...], 1, 1)
+    solved = thrice(split(top.T), split(k_ref[...]), 1, 0)
+    w_ref[...] = thrice(split(solved), split(p_ref[...]), 1, 1)
     lay(t_ref, m_ref[...])
     mine = pick(t_ref, col, 8, half, WIDTH, WIDTH)
     lay(t_ref, u_ref[...])

time: 95 us -> 93.5 us (0.984)
  Pallas kernels: 35.1 us -> 33.7 us
    pallas_call x1, Pallas kernels: 4.07 us -> 2.66 us  [make_weights(): pl.pallas_call(weights_kernel, out_shape=[jax.ShapeDtypeStruct((WIDTH //...]
  transfers between devices with their start and end apart: 17 -> 17, of which waited for: 6 -> 6; matrix products, arithmetic and copies ran while one was open for 1% -> 1% of each run, Pallas kernels for 27% -> 28%
where the time goes in v2:
time: 93.5 us; the launch traced here: 93.2 us
  starting transfers between devices  34.7 us (37%)
  Pallas kernels  33.7 us (36%)
  waiting for transfers between devices  21.3 us (23%)
  local copies, waits for them, and re-layouts  2.53 us (3%)
    ppermute x14, starting transfers between devices, shift(): return lax.ppermute(x, axis, ring(lax.axis_size(axis), step))  19.9 us
    ppermute x14, waiting for transfers between devices, shift(): return lax.ppermute(x, axis, ring(lax.axis_size(axis), step))  12.8 us
    all_to_all x1, starting transfers between devices, gather_tiles(): lax.all_to_all(jnp.broadcast_to(flat[None], (64,) + flat.shape), ('y', 'z...  12 us
    pallas_call x1, Pallas kernels, update_start(): pl.pallas_call(start_kernel, grid=(rows // tile,), out_shape=[jax.ShapeDt...  11.6 us
    all_to_all x1, waiting for transfers between devices, gather_tiles(): lax.all_to_all(jnp.broadcast_to(flat[None], (64,) + flat.shape), ('y', 'z...  8.5 us
    pallas_call x1, Pallas kernels, factor_first(): pl.pallas_call(first_half_kernel, out_shape=SQUARES, in_specs=[VMEM] * 2,...  7.98 us
    pallas_call x1, Pallas kernels, factor_second(): pl.pallas_call(second_half_kernel, out_shape=SQUARES, in_specs=[VMEM] * 3...  6.44 us
    pallas_call x1, Pallas kernels, update_more(): pl.pallas_call(functools.partial(go_on_kernel, place=place), grid=(rows /...  5.04 us
  transfers between devices with their start and end apart: 17, of which 6 were waited for; matrix products, arithmetic and copies ran while one was open for 1% of the time, Pallas kernels for 28%

profile of v2, /device:TPU:1, one launch (start us, length us, event | category | flops | bytes accessed | tf_op | source)
XLA Modules:
  0.0 93.2 jit_solution(629314581179341826)
XLA Ops:
  0.6 0.7 fusion
  1.3 0.1 pad_maximum_fusion.2
  1.4 0.8 broadcast_in_dim.2
  2.3 12.0 %all-to-all-start = ((f32[64,16,128]{2,1,0:T(8,128)}), f32[64,16,128]{2,1,0:T(8,128)S(1)}, u32[]{:S(2)}, u32[]{:S(2)}) async-start(f32[64,16,128]{2,1,0:T(8,128)} %broadcast_in_dim.2), calls=%async_computation | async-start | bytes 1048576 | tf_op jit(solution)/shard_map/all_to_all | solution.py:373
  14.2 2.3 %collective-permute-start.3 = (f32[64,3072]{1,0:T(8,128)}, f32[64,3072]{1,0:T(8,128)S(1)}, u32[]{:S(2)}, u32[]{:S(2)}) collective-permute-start(f32[64,3072]{1,0:T(8,128)} %bitcast.4), channel_id=1, source_target_pairs={{0,6},{2,0},{4,2},{6,4},{1,7},{3,1},{5,3},{7,5},{8,14},{10,8},{12,... | collective-permute-start | bytes 2359304 | tf_op jit(solution)/shard_map/ppermute | solution.py:363
  16.5 0.0 collective-permute-start.2
  16.5 1.2 %collective-permute-start.1 = (f32[64,3072]{1,0:T(8,128)}, f32[64,3072]{1,0:T(8,128)S(1)}, u32[]{:S(2)}, u32[]{:S(2)}) collective-permute-start(f32[64,3072]{1,0:T(8,128)} %bitcast.6), channel_id=1, source_target_pairs={{0,1},{1,0},{2,3},{3,2},{4,5},{5,4},{6,7},{7,6},{8,9},{9,8},{10,11... | collective-permute-start | bytes 2359304 | tf_op jit(solution)/shard_map/ppermute | solution.py:363
  17.7 8.5 %all-to-all-done.mine_ref = f32[64,16,128]{2,1,0:T(8,128)S(1)} async-done(((f32[64,16,128]{2,1,0:T(8,128)}), f32[64,16,128]{2,1,0:T(8,128)S(1)}, u32[]{:S(2)}, u32[]{:S(2)}) %all-to-all-start) | async-done | bytes 524320 | tf_op jit(solution)/shard_map/all_to_all | solution.py:373
  26.2 3.6 %collective-permute-start = (f32[64,16,128]{2,1,0:T(8,128)S(1)}, f32[64,16,128]{2,1,0:T(8,128)S(1)}, u32[]{:S(2)}, u32[]{:S(2)}) collective-permute-start(f32[64,16,128]{2,1,0:T(8,128)S(1)} %all-to-all-done.mine_ref), channel_id=1, source_target_pairs={{0,8},{8,0},{1,9},{9,1},{2,10},{10,2},{3,11},{11,3},{4,12},{12,4},... | collective-permute-start | bytes 1572872 | tf_op jit(solution)/shard_map/ppermute | solution.py:363
  29.8 0.9 slice.24
  30.7 0.0 collective-permute-start.5
  30.7 0.6 collective-permute-done.other_ref
  31.4 2.9 %collective-permute-start.4 = (f32[64,384]{1,0:T(8,128)S(1)}, f32[64,384]{1,0:T(8,128)S(1)}, u32[]{:S(2)}, u32[]{:S(2)}) collective-permute-start(f32[64,384]{1,0:T(8,128)S(1)} %slice.24), channel_id=1, source_target_pairs={{0,0},{1,16},{2,32},{3,48},{4,64},{5,80},{6,96},{7,112},{8,1},{9,1... | collective-permute-start | bytes 294920 | tf_op jit(solution)/shard_map/ppermute | solution.py:396
  34.3 8.0 %factor_first.1 = (f32[512,512]{1,0:T(8,128)S(1)}, f32[512,512]{1,0:T(8,128)S(1)}, f32[512,512]{1,0:T(8,128)S(1)}) custom-call(f32[64,16,128]{2,1,0:T(8,128)S(1)} %all-to-all-done.mine_ref, f32[64,16,128]{2,1,0:T(8,128)S(1)} %collective-permute-done.other_ref), custom_call_target="tpu_custom_call" | custom-call | flops 1000000 | bytes 1000 | tf_op jit(solution)/shard_map/factor_first/pallas_call | solution.py:187
  42.3 0.0 collective-permute-done.3.refs_3_
  42.3 0.0 collective-permute-done.2.refs_2_
  42.3 0.0 collective-permute-done.1.refs_1_
  42.3 0.0 slice-start
  42.3 0.0 copy-start
  42.3 0.0 slice-start.1
  42.3 0.0 slice-start.2
  42.3 5.5 %collective-permute-start.8 = (f32[64,3072]{1,0:T(8,128)S(1)}, f32[64,3072]{1,0:T(8,128)S(1)}, u32[]{:S(2)}, u32[]{:S(2)}) collective-permute-start(f32[64,3072]{1,0:T(8,128)S(1)} %collective-permute-done.3.refs_3_), channel_id=1, source_target_pairs={{0,6},{2,0},{4,2},{6,4},{1,7},{3,1},{5,3},{7,5},{8,14},{10,8},{12,... | collective-permute-start | bytes 2359304 | tf_op jit(solution)/shard_map/ppermute | solution.py:363
  47.8 0.5 collective-permute-start.6
  48.4 0.0 collective-permute-start.7
  48.4 6.4 %factor_second.1 = (f32[512,512]{1,0:T(8,128)S(1)}, f32[512,512]{1,0:T(8,128)S(1)}, f32[512,512]{1,0:T(8,128)S(1)}) custom-call(f32[512,512]{1,0:T(8,128)S(1)} %get-tuple-element.44.r_in, f32[512,512]{1,0:T(8,128)S(1)} %get-tuple-element.45.u_in, f32[512,512]{1,0:T(8,128)S(1)} %get-tuple-element.46.m_in), custom_call_target="tpu_custom_call", output_to_operand_aliasing={{0}: (0, {}), {1}: (1, {}), {2}: (2, {})} | custom-call | flops 30000001024 | bytes 1000000 | tf_op jit(solution)/shard_map/factor_second/pallas_call | solution.py:204
  54.8 0.0 collective-permute-done.5
  54.9 0.0 collective-permute-done.4
  54.9 0.4 collective-permute-start.11
  55.3 1.4 %collective-permute-start.10 = (f32[2,64,384]{2,1,0:T(8,128)S(1)}, f32[2,64,384]{2,1,0:T(8,128)S(1)}, u32[]{:S(2)}, u32[]{:S(2)}) collective-permute-start(f32[2,64,384]{2,1,0:T(8,128)S(1)} %pad_maximum_fusion.1.p0_ref), channel_id=1, source_target_pairs={{0,64},{32,96},{64,0},{96,32},{1,65},{33,97},{65,1},{97,33},{2,66}... | collective-permute-start | bytes 589832 | tf_op jit(solution)/shard_map/ppermute | solution.py:363
  56.7 4.7 %collective-permute-done.11.p3_ref = f32[2,64,384]{2,1,0:T(8,128)S(1)} collective-permute-done((f32[2,64,384]{2,1,0:T(8,128)S(1)}, f32[2,64,384]{2,1,0:T(8,128)S(1)}, u32[]{:S(2)}, u32[]{:S(2)}) %collective-permute-start.11) | collective-permute-done | bytes 196640 | tf_op jit(solution)/shard_map/ppermute | solution.py:363
  61.4 0.0 collective-permute-start.9
  61.4 1.2 %collective-permute-done.10.p2_ref = f32[2,64,384]{2,1,0:T(8,128)S(1)} collective-permute-done((f32[2,64,384]{2,1,0:T(8,128)S(1)}, f32[2,64,384]{2,1,0:T(8,128)S(1)}, u32[]{:S(2)}, u32[]{:S(2)}) %collective-permute-start.10) | collective-permute-done | bytes 196640 | tf_op jit(solution)/shard_map/ppermute | solution.py:363
  62.6 5.0 %collective-permute-done.9.p1_ref = f32[2,64,384]{2,1,0:T(8,128)S(1)} collective-permute-done((f32[2,64,384]{2,1,0:T(8,128)S(1)}, f32[2,64,384]{2,1,0:T(8,128)S(1)}, u32[]{:S(2)}, u32[]{:S(2)}) %collective-permute-start.9) | collective-permute-done | bytes 196640 | tf_op jit(solution)/shard_map/ppermute | solution.py:363
  67.7 1.2 %collective-permute-done.7.refs_5_ = f32[64,3072]{1,0:T(8,128)S(1)} collective-permute-done((f32[64,3072]{1,0:T(8,128)S(1)}, f32[64,3072]{1,0:T(8,128)S(1)}, u32[]{:S(2)}, u32[]{:S(2)}) %collective-permute-start.7) | collective-permute-done | bytes 786464 | tf_op jit(solution)/shard_map/ppermute | solution.py:363
  68.8 0.0 collective-permute-done.8.refs_6_
  68.8 0.0 collective-permute-done.6.refs_4_
  68.9 2.7 %weights.1 = (f32[32,64]{1,0:T(8,128)}, f32[64,512]{1,0:T(8,128)S(1)}, f32[384,512]{1,0:T(8,128)S(1)}) custom-call(f32[512,512]{1,0:T(8,128)S(1)} %get-tuple-element.55.u_ref, f32[512,512]{1,0:T(8,128)S(1)} %get-tuple-element.56.m_ref, f32[2,64,384]{2,1,0:T(8,128)S(1)} %pad_maximum_fusion.1.p0_ref, f32[2,64,384]{2,1,0:T(8,128)S(1)} %collective-permute-done.9.p1_ref, ...), custom_call_target="tpu_custom_call" | custom-call | flops 1000000 | bytes 1000 | tf_op jit(solution)/shard_map/weights/pallas_call | solution.py:248
  71.5 1.1 %collective-permute-start.12 = (f32[384,512]{1,0:T(8,128)S(1)}, f32[384,512]{1,0:T(8,128)S(1)}, u32[]{:S(2)}, u32[]{:S(2)}) collective-permute-start(f32[384,512]{1,0:T(8,128)S(1)} %get-tuple-element.63.mine_ref), channel_id=1, source_target_pairs={{0,8},{8,0},{1,9},{9,1},{2,10},{10,2},{3,11},{11,3},{4,12},{12,4},... | collective-permute-start | bytes 2359304 | tf_op jit(solution)/shard_map/ppermute | solution.py:363
  72.7 1.1 %collective-permute-start.13 = (f32[64,1024]{1,0:T(8,128)S(1)}, f32[64,1024]{1,0:T(8,128)S(1)}, u32[]{:S(2)}, u32[]{:S(2)}) collective-permute-start(f32[64,1024]{1,0:T(8,128)S(1)} %slice.21), channel_id=1, source_target_pairs={{0,1},{1,0},{2,3},{3,2},{4,5},{5,4},{6,7},{7,6},{8,9},{9,8},{10,11... | collective-permute-start | bytes 786440 | tf_op jit(solution)/shard_map/ppermute | solution.py:363
  73.8 0.6 collective-permute-start.14
  74.5 2.0 %collective-permute-start.15 = (f32[64,1024]{1,0:T(8,128)S(1)}, f32[64,1024]{1,0:T(8,128)S(1)}, u32[]{:S(2)}, u32[]{:S(2)}) collective-permute-start(f32[64,1024]{1,0:T(8,128)S(1)} %slice.23), channel_id=1, source_target_pairs={{0,6},{2,0},{4,2},{6,4},{1,7},{3,1},{5,3},{7,5},{8,14},{10,8},{12,... | collective-permute-start | bytes 786440 | tf_op jit(solution)/shard_map/ppermute | solution.py:363
  76.5 0.0 collective-permute-done.12.other_ref
  76.5 11.6 %update_start.1 = (f32[64,3072]{1,0:T(8,128)S(1)}, f32[3072,768]{1,0:T(8,128)S(1)}, bf16[512,768]{1,0:T(8,128)(2,1)S(1)}, bf16[512,768]{1,0:T(8,128)(2,1)S(1)}) custom-call(f32[384,512]{1,0:T(8,128)S(1)} %get-tuple-element.63.mine_ref, f32[384,512]{1,0:T(8,128)S(1)} %collective-permute-done.12.other_ref, f32[64,512]{1,0:T(8,128)S(1)} %get-tuple-element.62.own_ref, ...), custom_call_target="tpu_custom_call" | custom-call | flops 8000000000 | bytes 10000000 | tf_op jit(solution)/shard_map/update_start/pallas_call | solution.py:319
  88.1 0.0 collective-permute-done.13
  88.1 0.0 collective-permute-done.14
  88.1 0.0 collective-permute-done.15
  88.1 0.1 pad_maximum_fusion.refs_0_
  88.2 5.0 %update_last.1 = (f32[64,3072]{1,0:T(8,128)}, f32[3072,768]{1,0:T(8,128)}) custom-call(f32[64,512]{1,0:T(8,128)S(1)} %get-tuple-element.62.own_ref, bf16[512,768]{1,0:T(8,128)(2,1)S(1)} %get-tuple-element.68.high_ref, bf16[512,768]{1,0:T(8,128)(2,1)S(1)} %get-tuple-element.69.low_ref, f32[64,3072]{1,0:T(8,128)S(1)} %pad_maximum_fusion.refs_0_, ...), custom_call_target="tpu_custom_call" | custom-call | flops 1000000000 | bytes 10000000 | tf_op jit(solution)/shard_map/update_last/pallas_call | solution.py:341
  (9 shorter events, 0.1 us)
Async XLA Ops:
  2.3 24.0 %all-to-all-start = ((f32[64,16,128]{2,1,0:T(8,128)}), f32[64,16,128]{2,1,0:T(8,128)S(1)}, u32[]{:S(2)}, u32[]{:S(2)}) async-start(f32[64,16,128]{2,1,0:T(8,128)} %broadcast_in_dim.2), calls=%async_computation | async-start | bytes 1048576 | tf_op jit(solution)/shard_map/all_to_all | solution.py:373
  14.2 28.0 %collective-permute-start.3 = (f32[64,3072]{1,0:T(8,128)}, f32[64,3072]{1,0:T(8,128)S(1)}, u32[]{:S(2)}, u32[]{:S(2)}) collective-permute-start(f32[64,3072]{1,0:T(8,128)} %bitcast.4), channel_id=1, source_target_pairs={{0,6},{2,0},{4,2},{6,4},{1,7},{3,1},{5,3},{7,5},{8,14},{10,8},{12,... | collective-permute-start | bytes 2359304 | tf_op jit(solution)/shard_map/ppermute | solution.py:363
  16.5 25.8 %collective-permute-start.2 = (f32[64,3072]{1,0:T(8,128)}, f32[64,3072]{1,0:T(8,128)S(1)}, u32[]{:S(2)}, u32[]{:S(2)}) collective-permute-start(f32[64,3072]{1,0:T(8,128)} %bitcast.5), channel_id=1, source_target_pairs={{0,2},{2,4},{4,6},{6,0},{1,3},{3,5},{5,7},{7,1},{8,10},{10,12},{12... | collective-permute-start | bytes 2359304 | tf_op jit(solution)/shard_map/ppermute | solution.py:363
  16.5 25.8 %collective-permute-start.1 = (f32[64,3072]{1,0:T(8,128)}, f32[64,3072]{1,0:T(8,128)S(1)}, u32[]{:S(2)}, u32[]{:S(2)}) collective-permute-start(f32[64,3072]{1,0:T(8,128)} %bitcast.6), channel_id=1, source_target_pairs={{0,1},{1,0},{2,3},{3,2},{4,5},{5,4},{6,7},{7,6},{8,9},{9,8},{10,11... | collective-permute-start | bytes 2359304 | tf_op jit(solution)/shard_map/ppermute | solution.py:363
  26.2 5.2 %collective-permute-start = (f32[64,16,128]{2,1,0:T(8,128)S(1)}, f32[64,16,128]{2,1,0:T(8,128)S(1)}, u32[]{:S(2)}, u32[]{:S(2)}) collective-permute-start(f32[64,16,128]{2,1,0:T(8,128)S(1)} %all-to-all-done.mine_ref), channel_id=1, source_target_pairs={{0,8},{8,0},{1,9},{9,1},{2,10},{10,2},{3,11},{11,3},{4,12},{12,4},... | collective-permute-start | bytes 1572872 | tf_op jit(solution)/shard_map/ppermute | solution.py:363
  30.7 24.1 %collective-permute-start.5 = (f32[64,384]{1,0:T(8,128)S(1)}, f32[64,384]{1,0:T(8,128)S(1)}, u32[]{:S(2)}, u32[]{:S(2)}) collective-permute-start(f32[64,384]{1,0:T(8,128)S(1)} %slice.24), channel_id=1, source_target_pairs={{0,16},{1,0},{2,48},{3,32},{4,80},{5,64},{6,112},{7,96},{8,17},{9,... | collective-permute-start | bytes 294920 | tf_op jit(solution)/shard_map/ppermute | solution.py:396
  31.4 23.5 %collective-permute-start.4 = (f32[64,384]{1,0:T(8,128)S(1)}, f32[64,384]{1,0:T(8,128)S(1)}, u32[]{:S(2)}, u32[]{:S(2)}) collective-permute-start(f32[64,384]{1,0:T(8,128)S(1)} %slice.24), channel_id=1, source_target_pairs={{0,0},{1,16},{2,32},{3,48},{4,64},{5,80},{6,96},{7,112},{8,1},{9,1... | collective-permute-start | bytes 294920 | tf_op jit(solution)/shard_map/ppermute | solution.py:396
  42.3 34.2 %slice-start = ((s8[9437184]{0:T(1024)(128)(4,1)}), s8[4194304]{0:T(1024)(128)(4,1)S(1)}, s32[]{:S(2)}) async-start(s8[9437184]{0:T(1024)(128)(4,1)} %bitcast.9), calls=%async_computation.1 | async-start | bytes 8388608
  42.3 34.2 %copy-start = (f32[3072,64]{0,1:T(8,128)S(1)}, f32[3072,64]{0,1:T(8,128)}, u32[]{:S(2)}) copy-start(f32[3072,64]{0,1:T(8,128)} %param.4) | copy-start | bytes 2359300
  42.3 34.2 %slice-start.1 = ((s8[9437184]{0:T(1024)(128)(4,1)}), s8[4194304]{0:T(1024)(128)(4,1)S(1)}, s32[]{:S(2)}) async-start(s8[9437184]{0:T(1024)(128)(4,1)} %bitcast.9), calls=%async_computation.2 | async-start | bytes 8388608
  42.3 34.2 %slice-start.2 = ((s8[9437184]{0:T(1024)(128)(4,1)}), s8[1048576]{0:T(1024)(128)(4,1)S(1)}, s32[]{:S(2)}) async-start(s8[9437184]{0:T(1024)(128)(4,1)} %bitcast.9), calls=%async_computation.3 | async-start | bytes 2097152
  42.3 26.5 %collective-permute-start.8 = (f32[64,3072]{1,0:T(8,128)S(1)}, f32[64,3072]{1,0:T(8,128)S(1)}, u32[]{:S(2)}, u32[]{:S(2)}) collective-permute-start(f32[64,3072]{1,0:T(8,128)S(1)} %collective-permute-done.3.refs_3_), channel_id=1, source_target_pairs={{0,6},{2,0},{4,2},{6,4},{1,7},{3,1},{5,3},{7,5},{8,14},{10,8},{12,... | collective-permute-start | bytes 2359304 | tf_op jit(solution)/shard_map/ppermute | solution.py:363
  47.8 21.0 %collective-permute-start.6 = (f32[64,3072]{1,0:T(8,128)S(1)}, f32[64,3072]{1,0:T(8,128)S(1)}, u32[]{:S(2)}, u32[]{:S(2)}) collective-permute-start(f32[64,3072]{1,0:T(8,128)S(1)} %collective-permute-done.3.refs_3_), channel_id=1, source_target_pairs={{0,1},{1,0},{2,3},{3,2},{4,5},{5,4},{6,7},{7,6},{8,9},{9,8},{10,11... | collective-permute-start | bytes 2359304 | tf_op jit(solution)/shard_map/ppermute | solution.py:363
  48.4 20.5 %collective-permute-start.7 = (f32[64,3072]{1,0:T(8,128)S(1)}, f32[64,3072]{1,0:T(8,128)S(1)}, u32[]{:S(2)}, u32[]{:S(2)}) collective-permute-start(f32[64,3072]{1,0:T(8,128)S(1)} %collective-permute-done.1.refs_1_), channel_id=1, source_target_pairs={{0,2},{2,4},{4,6},{6,0},{1,3},{3,5},{5,7},{7,1},{8,10},{10,12},{12... | collective-permute-start | bytes 2359304 | tf_op jit(solution)/shard_map/ppermute | solution.py:363
  54.9 6.5 %collective-permute-start.11 = (f32[2,64,384]{2,1,0:T(8,128)S(1)}, f32[2,64,384]{2,1,0:T(8,128)S(1)}, u32[]{:S(2)}, u32[]{:S(2)}) collective-permute-start(f32[2,64,384]{2,1,0:T(8,128)S(1)} %pad_maximum_fusion.1.p0_ref), channel_id=1, source_target_pairs={{0,96},{32,0},{64,32},{96,64},{1,97},{33,1},{65,33},{97,65},{2,98}... | collective-permute-start | bytes 589832 | tf_op jit(solution)/shard_map/ppermute | solution.py:363
  55.3 7.3 %collective-permute-start.10 = (f32[2,64,384]{2,1,0:T(8,128)S(1)}, f32[2,64,384]{2,1,0:T(8,128)S(1)}, u32[]{:S(2)}, u32[]{:S(2)}) collective-permute-start(f32[2,64,384]{2,1,0:T(8,128)S(1)} %pad_maximum_fusion.1.p0_ref), channel_id=1, source_target_pairs={{0,64},{32,96},{64,0},{96,32},{1,65},{33,97},{65,1},{97,33},{2,66}... | collective-permute-start | bytes 589832 | tf_op jit(solution)/shard_map/ppermute | solution.py:363
  61.4 6.3 %collective-permute-start.9 = (f32[2,64,384]{2,1,0:T(8,128)S(1)}, f32[2,64,384]{2,1,0:T(8,128)S(1)}, u32[]{:S(2)}, u32[]{:S(2)}) collective-permute-start(f32[2,64,384]{2,1,0:T(8,128)S(1)} %pad_maximum_fusion.1.p0_ref), channel_id=1, source_target_pairs={{0,32},{32,64},{64,96},{96,0},{1,33},{33,65},{65,97},{97,1},{2,34}... | collective-permute-start | bytes 589832 | tf_op jit(solution)/shard_map/ppermute | solution.py:363
  71.5 5.0 %collective-permute-start.12 = (f32[384,512]{1,0:T(8,128)S(1)}, f32[384,512]{1,0:T(8,128)S(1)}, u32[]{:S(2)}, u32[]{:S(2)}) collective-permute-start(f32[384,512]{1,0:T(8,128)S(1)} %get-tuple-element.63.mine_ref), channel_id=1, source_target_pairs={{0,8},{8,0},{1,9},{9,1},{2,10},{10,2},{3,11},{11,3},{4,12},{12,4},... | collective-permute-start | bytes 2359304 | tf_op jit(solution)/shard_map/ppermute | solution.py:363
  72.7 15.4 %collective-permute-start.13 = (f32[64,1024]{1,0:T(8,128)S(1)}, f32[64,1024]{1,0:T(8,128)S(1)}, u32[]{:S(2)}, u32[]{:S(2)}) collective-permute-start(f32[64,1024]{1,0:T(8,128)S(1)} %slice.21), channel_id=1, source_target_pairs={{0,1},{1,0},{2,3},{3,2},{4,5},{5,4},{6,7},{7,6},{8,9},{9,8},{10,11... | collective-permute-start | bytes 786440 | tf_op jit(solution)/shard_map/ppermute | solution.py:363
  73.8 14.3 %collective-permute-start.14 = (f32[64,1024]{1,0:T(8,128)S(1)}, f32[64,1024]{1,0:T(8,128)S(1)}, u32[]{:S(2)}, u32[]{:S(2)}) collective-permute-start(f32[64,1024]{1,0:T(8,128)S(1)} %slice.22), channel_id=1, source_target_pairs={{0,2},{2,4},{4,6},{6,0},{1,3},{3,5},{5,7},{7,1},{8,10},{10,12},{12... | collective-permute-start | bytes 786440 | tf_op jit(solution)/shard_map/ppermute | solution.py:363
  74.5 13.7 %collective-permute-start.15 = (f32[64,1024]{1,0:T(8,128)S(1)}, f32[64,1024]{1,0:T(8,128)S(1)}, u32[]{:S(2)}, u32[]{:S(2)}) collective-permute-start(f32[64,1024]{1,0:T(8,128)S(1)} %slice.23), channel_id=1, source_target_pairs={{0,6},{2,0},{4,2},{6,4},{1,7},{3,1},{5,3},{7,5},{8,14},{10,8},{12,... | collective-permute-start | bytes 786440 | tf_op jit(solution)/shard_map/ppermute | solution.py:363

commit v3 on v2

--- a/solution.py
+++ b/solution.py
@@ -408,12 +408,8 @@
         upper, inverse, from_rz, from_lz, from_2, *pairs
     )
     diag_factor, own, weights = make_weights(upper, inverse, pairs)
-    third = panel_t.shape[1] // 3
-    parts = (
-        shift(from_2[:, :third], "zl", 1),
-        shift(from_lz[:, third : 2 * third], "x", 1),
-        shift(from_rz[:, 2 * third :], "x", -1),
-    )
+    half = panel_t.shape[1] // 2
+    parts = (shift(from_lz[:, :half], "x", 1), shift(from_rz[:, half:], "x", -1))
     weights_other = shift(weights, "core", 1)
     blocks = [panel_t, from_z, from_l, from_r, from_rz, from_lz, from_2]
     factor_part, rest, high, low = update_start(weights, weights_other, own, blocks, trailing)

time: 93.5 us -> 92.7 us (level)
    ppermute x14 -> x13, starting transfers between devices: 19.9 us -> 19 us  [shift(): return lax.ppermute(x, axis, ring(lax.axis_size(axis), step))]
    ppermute x14 -> x13, waiting for transfers between devices: 12.8 us -> 12.8 us  [shift(): return lax.ppermute(x, axis, ring(lax.axis_size(axis), step))]
  transfers between devices with their start and end apart: 17 -> 16, of which waited for: 6 -> 6; matrix products, arithmetic and copies ran while one was open for 1% -> 1% of each run, Pallas kernels for 28% -> 28%
where the time goes in v3:
time: 92.7 us; the launch traced here: 92.4 us
  starting transfers between devices  33.9 us (37%)
  Pallas kernels  33.7 us (36%)
  waiting for transfers between devices  21.3 us (23%)
  local copies, waits for them, and re-layouts  2.52 us (3%)
    ppermute x13, starting transfers between devices, shift(): return lax.ppermute(x, axis, ring(lax.axis_size(axis), step))  19 us
    ppermute x13, waiting for transfers between devices, shift(): return lax.ppermute(x, axis, ring(lax.axis_size(axis), step))  12.8 us
    all_to_all x1, starting transfers between devices, gather_tiles(): lax.all_to_all(jnp.broadcast_to(flat[None], (64,) + flat.shape), ('y', 'z...  12 us
    pallas_call x1, Pallas kernels, update_start(): pl.pallas_call(start_kernel, grid=(rows // tile,), out_shape=[jax.ShapeDt...  11.5 us
    all_to_all x1, waiting for transfers between devices, gather_tiles(): lax.all_to_all(jnp.broadcast_to(flat[None], (64,) + flat.shape), ('y', 'z...  8.5 us
    pallas_call x1, Pallas kernels, factor_first(): pl.pallas_call(first_half_kernel, out_shape=SQUARES, in_specs=[VMEM] * 2,...  7.98 us
    pallas_call x1, Pallas kernels, factor_second(): pl.pallas_call(second_half_kernel, out_shape=SQUARES, in_specs=[VMEM] * 3...  6.44 us
    pallas_call x1, Pallas kernels, update_more(): pl.pallas_call(functools.partial(go_on_kernel, place=place), grid=(rows /...  5.04 us
  transfers between devices with their start and end apart: 16, of which 6 were waited for; matrix products, arithmetic and copies ran while one was open for 1% of the time, Pallas kernels for 28%

profile of v3, /device:TPU:1, one launch (start us, length us, event | category | flops | bytes accessed | tf_op | source)
XLA Modules:
  0.0 92.4 jit_solution(1082905999480370910)
XLA Ops:
  0.6 0.7 fusion
  1.3 0.1 pad_maximum_fusion.2
  1.4 0.8 broadcast_in_dim.2
  2.3 12.0 %all-to-all-start = ((f32[64,16,128]{2,1,0:T(8,128)}), f32[64,16,128]{2,1,0:T(8,128)S(1)}, u32[]{:S(2)}, u32[]{:S(2)}) async-start(f32[64,16,128]{2,1,0:T(8,128)} %broadcast_in_dim.2), calls=%async_computation | async-start | bytes 1048576 | tf_op jit(solution)/shard_map/all_to_all | solution.py:373
  14.2 2.3 %collective-permute-start.3 = (f32[64,3072]{1,0:T(8,128)}, f32[64,3072]{1,0:T(8,128)S(1)}, u32[]{:S(2)}, u32[]{:S(2)}) collective-permute-start(f32[64,3072]{1,0:T(8,128)} %bitcast.4), channel_id=1, source_target_pairs={{0,6},{2,0},{4,2},{6,4},{1,7},{3,1},{5,3},{7,5},{8,14},{10,8},{12,... | collective-permute-start | bytes 2359304 | tf_op jit(solution)/shard_map/ppermute | solution.py:363
  16.5 0.0 collective-permute-start.2
  16.5 1.2 %collective-permute-start.1 = (f32[64,3072]{1,0:T(8,128)}, f32[64,3072]{1,0:T(8,128)S(1)}, u32[]{:S(2)}, u32[]{:S(2)}) collective-permute-start(f32[64,3072]{1,0:T(8,128)} %bitcast.6), channel_id=1, source_target_pairs={{0,1},{1,0},{2,3},{3,2},{4,5},{5,4},{6,7},{7,6},{8,9},{9,8},{10,11... | collective-permute-start | bytes 2359304 | tf_op jit(solution)/shard_map/ppermute | solution.py:363
  17.7 8.5 %all-to-all-done.mine_ref = f32[64,16,128]{2,1,0:T(8,128)S(1)} async-done(((f32[64,16,128]{2,1,0:T(8,128)}), f32[64,16,128]{2,1,0:T(8,128)S(1)}, u32[]{:S(2)}, u32[]{:S(2)}) %all-to-all-start) | async-done | bytes 524320 | tf_op jit(solution)/shard_map/all_to_all | solution.py:373
  26.2 3.6 %collective-permute-start = (f32[64,16,128]{2,1,0:T(8,128)S(1)}, f32[64,16,128]{2,1,0:T(8,128)S(1)}, u32[]{:S(2)}, u32[]{:S(2)}) collective-permute-start(f32[64,16,128]{2,1,0:T(8,128)S(1)} %all-to-all-done.mine_ref), channel_id=1, source_target_pairs={{0,8},{8,0},{1,9},{9,1},{2,10},{10,2},{3,11},{11,3},{4,12},{12,4},... | collective-permute-start | bytes 1572872 | tf_op jit(solution)/shard_map/ppermute | solution.py:363
  29.8 0.9 slice.20
  30.7 0.0 collective-permute-start.5
  30.7 0.6 collective-permute-done.other_ref
  31.4 2.9 %collective-permute-start.4 = (f32[64,384]{1,0:T(8,128)S(1)}, f32[64,384]{1,0:T(8,128)S(1)}, u32[]{:S(2)}, u32[]{:S(2)}) collective-permute-start(f32[64,384]{1,0:T(8,128)S(1)} %slice.20), channel_id=1, source_target_pairs={{0,0},{1,16},{2,32},{3,48},{4,64},{5,80},{6,96},{7,112},{8,1},{9,1... | collective-permute-start | bytes 294920 | tf_op jit(solution)/shard_map/ppermute | solution.py:396
  34.3 8.0 %factor_first.1 = (f32[512,512]{1,0:T(8,128)S(1)}, f32[512,512]{1,0:T(8,128)S(1)}, f32[512,512]{1,0:T(8,128)S(1)}) custom-call(f32[64,16,128]{2,1,0:T(8,128)S(1)} %all-to-all-done.mine_ref, f32[64,16,128]{2,1,0:T(8,128)S(1)} %collective-permute-done.other_ref), custom_call_target="tpu_custom_call" | custom-call | flops 1000000 | bytes 1000 | tf_op jit(solution)/shard_map/factor_first/pallas_call | solution.py:187
  42.3 0.0 collective-permute-done.3.refs_3_
  42.3 0.0 collective-permute-done.2.refs_2_
  42.3 0.0 collective-permute-done.1.refs_1_
  42.3 0.0 slice-start
  42.3 0.0 copy-start
  42.3 0.0 slice-start.1
  42.3 0.0 slice-start.2
  42.3 5.5 %collective-permute-start.8 = (f32[64,3072]{1,0:T(8,128)S(1)}, f32[64,3072]{1,0:T(8,128)S(1)}, u32[]{:S(2)}, u32[]{:S(2)}) collective-permute-start(f32[64,3072]{1,0:T(8,128)S(1)} %collective-permute-done.3.refs_3_), channel_id=1, source_target_pairs={{0,6},{2,0},{4,2},{6,4},{1,7},{3,1},{5,3},{7,5},{8,14},{10,8},{12,... | collective-permute-start | bytes 2359304 | tf_op jit(solution)/shard_map/ppermute | solution.py:363
  47.8 0.5 collective-permute-start.6
  48.4 0.0 collective-permute-start.7
  48.4 6.4 %factor_second.1 = (f32[512,512]{1,0:T(8,128)S(1)}, f32[512,512]{1,0:T(8,128)S(1)}, f32[512,512]{1,0:T(8,128)S(1)}) custom-call(f32[512,512]{1,0:T(8,128)S(1)} %get-tuple-element.43.r_in, f32[512,512]{1,0:T(8,128)S(1)} %get-tuple-element.44.u_in, f32[512,512]{1,0:T(8,128)S(1)} %get-tuple-element.45.m_in), custom_call_target="tpu_custom_call", output_to_operand_aliasing={{0}: (0, {}), {1}: (1, {}), {2}: (2, {})} | custom-call | flops 30000001024 | bytes 1000000 | tf_op jit(solution)/shard_map/factor_second/pallas_call | solution.py:204
  54.8 0.0 collective-permute-done.5
  54.9 0.0 collective-permute-done.4
  54.9 0.4 collective-permute-start.11
  55.3 1.4 %collective-permute-start.10 = (f32[2,64,384]{2,1,0:T(8,128)S(1)}, f32[2,64,384]{2,1,0:T(8,128)S(1)}, u32[]{:S(2)}, u32[]{:S(2)}) collective-permute-start(f32[2,64,384]{2,1,0:T(8,128)S(1)} %pad_maximum_fusion.1.p0_ref), channel_id=1, source_target_pairs={{0,64},{32,96},{64,0},{96,32},{1,65},{33,97},{65,1},{97,33},{2,66}... | collective-permute-start | bytes 589832 | tf_op jit(solution)/shard_map/ppermute | solution.py:363
  56.7 4.7 %collective-permute-done.11.p3_ref = f32[2,64,384]{2,1,0:T(8,128)S(1)} collective-permute-done((f32[2,64,384]{2,1,0:T(8,128)S(1)}, f32[2,64,384]{2,1,0:T(8,128)S(1)}, u32[]{:S(2)}, u32[]{:S(2)}) %collective-permute-start.11) | collective-permute-done | bytes 196640 | tf_op jit(solution)/shard_map/ppermute | solution.py:363
  61.4 0.0 collective-permute-start.9
  61.4 1.2 %collective-permute-done.10.p2_ref = f32[2,64,384]{2,1,0:T(8,128)S(1)} collective-permute-done((f32[2,64,384]{2,1,0:T(8,128)S(1)}, f32[2,64,384]{2,1,0:T(8,128)S(1)}, u32[]{:S(2)}, u32[]{:S(2)}) %collective-permute-start.10) | collective-permute-done | bytes 196640 | tf_op jit(solution)/shard_map/ppermute | solution.py:363
  62.6 5.0 %collective-permute-done.9.p1_ref = f32[2,64,384]{2,1,0:T(8,128)S(1)} collective-permute-done((f32[2,64,384]{2,1,0:T(8,128)S(1)}, f32[2,64,384]{2,1,0:T(8,128)S(1)}, u32[]{:S(2)}, u32[]{:S(2)}) %collective-permute-start.9) | collective-permute-done | bytes 196640 | tf_op jit(solution)/shard_map/ppermute | solution.py:363
  67.7 1.2 %collective-permute-done.7.refs_5_ = f32[64,3072]{1,0:T(8,128)S(1)} collective-permute-done((f32[64,3072]{1,0:T(8,128)S(1)}, f32[64,3072]{1,0:T(8,128)S(1)}, u32[]{:S(2)}, u32[]{:S(2)}) %collective-permute-start.7) | collective-permute-done | bytes 786464 | tf_op jit(solution)/shard_map/ppermute | solution.py:363
  68.8 0.0 collective-permute-done.8.refs_6_
  68.8 0.0 collective-permute-done.6.refs_4_
  68.9 2.7 %weights.1 = (f32[32,64]{1,0:T(8,128)}, f32[64,512]{1,0:T(8,128)S(1)}, f32[384,512]{1,0:T(8,128)S(1)}) custom-call(f32[512,512]{1,0:T(8,128)S(1)} %get-tuple-element.54.u_ref, f32[512,512]{1,0:T(8,128)S(1)} %get-tuple-element.55.m_ref, f32[2,64,384]{2,1,0:T(8,128)S(1)} %pad_maximum_fusion.1.p0_ref, f32[2,64,384]{2,1,0:T(8,128)S(1)} %collective-permute-done.9.p1_ref, ...), custom_call_target="tpu_custom_call" | custom-call | flops 1000000 | bytes 1000 | tf_op jit(solution)/shard_map/weights/pallas_call | solution.py:248
  71.5 1.1 %collective-permute-start.12 = (f32[384,512]{1,0:T(8,128)S(1)}, f32[384,512]{1,0:T(8,128)S(1)}, u32[]{:S(2)}, u32[]{:S(2)}) collective-permute-start(f32[384,512]{1,0:T(8,128)S(1)} %get-tuple-element.62.mine_ref), channel_id=1, source_target_pairs={{0,8},{8,0},{1,9},{9,1},{2,10},{10,2},{3,11},{11,3},{4,12},{12,4},... | collective-permute-start | bytes 2359304 | tf_op jit(solution)/shard_map/ppermute | solution.py:363
  72.7 0.6 collective-permute-start.13
  73.3 2.3 %collective-permute-start.14 = (f32[64,1536]{1,0:T(8,128)S(1)}, f32[64,1536]{1,0:T(8,128)S(1)}, u32[]{:S(2)}, u32[]{:S(2)}) collective-permute-start(f32[64,1536]{1,0:T(8,128)S(1)} %slice.19), channel_id=1, source_target_pairs={{0,6},{2,0},{4,2},{6,4},{1,7},{3,1},{5,3},{7,5},{8,14},{10,8},{12,... | collective-permute-start | bytes 1179656 | tf_op jit(solution)/shard_map/ppermute | solution.py:363
  75.6 0.0 collective-permute-done.12.other_ref
  75.6 0.0 slice-done
  75.7 0.0 copy-done
  75.7 11.5 %update_start.1 = (f32[64,3072]{1,0:T(8,128)S(1)}, f32[3072,768]{1,0:T(8,128)S(1)}, bf16[512,768]{1,0:T(8,128)(2,1)S(1)}, bf16[512,768]{1,0:T(8,128)(2,1)S(1)}) custom-call(f32[384,512]{1,0:T(8,128)S(1)} %get-tuple-element.62.mine_ref, f32[384,512]{1,0:T(8,128)S(1)} %collective-permute-done.12.other_ref, f32[64,512]{1,0:T(8,128)S(1)} %get-tuple-element.61.own_ref, ...), custom_call_target="tpu_custom_call" | custom-call | flops 8000000000 | bytes 10000000 | tf_op jit(solution)/shard_map/update_start/pallas_call | solution.py:319
  87.2 0.0 collective-permute-done.13
  87.3 0.0 collective-permute-done.14
  87.3 0.1 pad_maximum_fusion.refs_0_
  87.3 5.0 %update_last.1 = (f32[64,3072]{1,0:T(8,128)}, f32[3072,768]{1,0:T(8,128)}) custom-call(f32[64,512]{1,0:T(8,128)S(1)} %get-tuple-element.61.own_ref, bf16[512,768]{1,0:T(8,128)(2,1)S(1)} %get-tuple-element.67.high_ref, bf16[512,768]{1,0:T(8,128)(2,1)S(1)} %get-tuple-element.68.low_ref, f32[64,3072]{1,0:T(8,128)S(1)} %pad_maximum_fusion.refs_0_, ...), custom_call_target="tpu_custom_call" | custom-call | flops 1000000000 | bytes 10000000 | tf_op jit(solution)/shard_map/update_last/pallas_call | solution.py:341
  (6 shorter events, 0.1 us)
Async XLA Ops:
  2.3 24.0 %all-to-all-start = ((f32[64,16,128]{2,1,0:T(8,128)}), f32[64,16,128]{2,1,0:T(8,128)S(1)}, u32[]{:S(2)}, u32[]{:S(2)}) async-start(f32[64,16,128]{2,1,0:T(8,128)} %broadcast_in_dim.2), calls=%async_computation | async-start | bytes 1048576 | tf_op jit(solution)/shard_map/all_to_all | solution.py:373
  14.2 28.0 %collective-permute-start.3 = (f32[64,3072]{1,0:T(8,128)}, f32[64,3072]{1,0:T(8,128)S(1)}, u32[]{:S(2)}, u32[]{:S(2)}) collective-permute-start(f32[64,3072]{1,0:T(8,128)} %bitcast.4), channel_id=1, source_target_pairs={{0,6},{2,0},{4,2},{6,4},{1,7},{3,1},{5,3},{7,5},{8,14},{10,8},{12,... | collective-permute-start | bytes 2359304 | tf_op jit(solution)/shard_map/ppermute | solution.py:363
  16.5 25.8 %collective-permute-start.2 = (f32[64,3072]{1,0:T(8,128)}, f32[64,3072]{1,0:T(8,128)S(1)}, u32[]{:S(2)}, u32[]{:S(2)}) collective-permute-start(f32[64,3072]{1,0:T(8,128)} %bitcast.5), channel_id=1, source_target_pairs={{0,2},{2,4},{4,6},{6,0},{1,3},{3,5},{5,7},{7,1},{8,10},{10,12},{12... | collective-permute-start | bytes 2359304 | tf_op jit(solution)/shard_map/ppermute | solution.py:363
  16.5 25.8 %collective-permute-start.1 = (f32[64,3072]{1,0:T(8,128)}, f32[64,3072]{1,0:T(8,128)S(1)}, u32[]{:S(2)}, u32[]{:S(2)}) collective-permute-start(f32[64,3072]{1,0:T(8,128)} %bitcast.6), channel_id=1, source_target_pairs={{0,1},{1,0},{2,3},{3,2},{4,5},{5,4},{6,7},{7,6},{8,9},{9,8},{10,11... | collective-permute-start | bytes 2359304 | tf_op jit(solution)/shard_map/ppermute | solution.py:363
  26.2 5.2 %collective-permute-start = (f32[64,16,128]{2,1,0:T(8,128)S(1)}, f32[64,16,128]{2,1,0:T(8,128)S(1)}, u32[]{:S(2)}, u32[]{:S(2)}) collective-permute-start(f32[64,16,128]{2,1,0:T(8,128)S(1)} %all-to-all-done.mine_ref), channel_id=1, source_target_pairs={{0,8},{8,0},{1,9},{9,1},{2,10},{10,2},{3,11},{11,3},{4,12},{12,4},... | collective-permute-start | bytes 1572872 | tf_op jit(solution)/shard_map/ppermute | solution.py:363
  30.7 24.1 %collective-permute-start.5 = (f32[64,384]{1,0:T(8,128)S(1)}, f32[64,384]{1,0:T(8,128)S(1)}, u32[]{:S(2)}, u32[]{:S(2)}) collective-permute-start(f32[64,384]{1,0:T(8,128)S(1)} %slice.20), channel_id=1, source_target_pairs={{0,16},{1,0},{2,48},{3,32},{4,80},{5,64},{6,112},{7,96},{8,17},{9,... | collective-permute-start | bytes 294920 | tf_op jit(solution)/shard_map/ppermute | solution.py:396
  31.4 23.5 %collective-permute-start.4 = (f32[64,384]{1,0:T(8,128)S(1)}, f32[64,384]{1,0:T(8,128)S(1)}, u32[]{:S(2)}, u32[]{:S(2)}) collective-permute-start(f32[64,384]{1,0:T(8,128)S(1)} %slice.20), channel_id=1, source_target_pairs={{0,0},{1,16},{2,32},{3,48},{4,64},{5,80},{6,96},{7,112},{8,1},{9,1... | collective-permute-start | bytes 294920 | tf_op jit(solution)/shard_map/ppermute | solution.py:396
  42.3 33.4 %slice-start = ((s8[9437184]{0:T(1024)(128)(4,1)}), s8[4194304]{0:T(1024)(128)(4,1)S(1)}, s32[]{:S(2)}) async-start(s8[9437184]{0:T(1024)(128)(4,1)} %bitcast.9), calls=%async_computation.1 | async-start | bytes 8388608
  42.3 33.3 %copy-start = (f32[3072,64]{0,1:T(8,128)S(1)}, f32[3072,64]{0,1:T(8,128)}, u32[]{:S(2)}) copy-start(f32[3072,64]{0,1:T(8,128)} %param.4) | copy-start | bytes 2359300
  42.3 33.3 %slice-start.1 = ((s8[9437184]{0:T(1024)(128)(4,1)}), s8[4194304]{0:T(1024)(128)(4,1)S(1)}, s32[]{:S(2)}) async-start(s8[9437184]{0:T(1024)(128)(4,1)} %bitcast.9), calls=%async_computation.2 | async-start | bytes 8388608
  42.3 33.3 %slice-start.2 = ((s8[9437184]{0:T(1024)(128)(4,1)}), s8[1048576]{0:T(1024)(128)(4,1)S(1)}, s32[]{:S(2)}) async-start(s8[9437184]{0:T(1024)(128)(4,1)} %bitcast.9), calls=%async_computation.3 | async-start | bytes 2097152
  42.3 26.5 %collective-permute-start.8 = (f32[64,3072]{1,0:T(8,128)S(1)}, f32[64,3072]{1,0:T(8,128)S(1)}, u32[]{:S(2)}, u32[]{:S(2)}) collective-permute-start(f32[64,3072]{1,0:T(8,128)S(1)} %collective-permute-done.3.refs_3_), channel_id=1, source_target_pairs={{0,6},{2,0},{4,2},{6,4},{1,7},{3,1},{5,3},{7,5},{8,14},{10,8},{12,... | collective-permute-start | bytes 2359304 | tf_op jit(solution)/shard_map/ppermute | solution.py:363
  47.8 21.0 %collective-permute-start.6 = (f32[64,3072]{1,0:T(8,128)S(1)}, f32[64,3072]{1,0:T(8,128)S(1)}, u32[]{:S(2)}, u32[]{:S(2)}) collective-permute-start(f32[64,3072]{1,0:T(8,128)S(1)} %collective-permute-done.3.refs_3_), channel_id=1, source_target_pairs={{0,1},{1,0},{2,3},{3,2},{4,5},{5,4},{6,7},{7,6},{8,9},{9,8},{10,11... | collective-permute-start | bytes 2359304 | tf_op jit(solution)/shard_map/ppermute | solution.py:363
  48.4 20.5 %collective-permute-start.7 = (f32[64,3072]{1,0:T(8,128)S(1)}, f32[64,3072]{1,0:T(8,128)S(1)}, u32[]{:S(2)}, u32[]{:S(2)}) collective-permute-start(f32[64,3072]{1,0:T(8,128)S(1)} %collective-permute-done.1.refs_1_), channel_id=1, source_target_pairs={{0,2},{2,4},{4,6},{6,0},{1,3},{3,5},{5,7},{7,1},{8,10},{10,12},{12... | collective-permute-start | bytes 2359304 | tf_op jit(solution)/shard_map/ppermute | solution.py:363
  54.9 6.5 %collective-permute-start.11 = (f32[2,64,384]{2,1,0:T(8,128)S(1)}, f32[2,64,384]{2,1,0:T(8,128)S(1)}, u32[]{:S(2)}, u32[]{:S(2)}) collective-permute-start(f32[2,64,384]{2,1,0:T(8,128)S(1)} %pad_maximum_fusion.1.p0_ref), channel_id=1, source_target_pairs={{0,96},{32,0},{64,32},{96,64},{1,97},{33,1},{65,33},{97,65},{2,98}... | collective-permute-start | bytes 589832 | tf_op jit(solution)/shard_map/ppermute | solution.py:363
  55.3 7.3 %collective-permute-start.10 = (f32[2,64,384]{2,1,0:T(8,128)S(1)}, f32[2,64,384]{2,1,0:T(8,128)S(1)}, u32[]{:S(2)}, u32[]{:S(2)}) collective-permute-start(f32[2,64,384]{2,1,0:T(8,128)S(1)} %pad_maximum_fusion.1.p0_ref), channel_id=1, source_target_pairs={{0,64},{32,96},{64,0},{96,32},{1,65},{33,97},{65,1},{97,33},{2,66}... | collective-permute-start | bytes 589832 | tf_op jit(solution)/shard_map/ppermute | solution.py:363
  61.4 6.3 %collective-permute-start.9 = (f32[2,64,384]{2,1,0:T(8,128)S(1)}, f32[2,64,384]{2,1,0:T(8,128)S(1)}, u32[]{:S(2)}, u32[]{:S(2)}) collective-permute-start(f32[2,64,384]{2,1,0:T(8,128)S(1)} %pad_maximum_fusion.1.p0_ref), channel_id=1, source_target_pairs={{0,32},{32,64},{64,96},{96,0},{1,33},{33,65},{65,97},{97,1},{2,34}... | collective-permute-start | bytes 589832 | tf_op jit(solution)/shard_map/ppermute | solution.py:363
  71.5 4.1 %collective-permute-start.12 = (f32[384,512]{1,0:T(8,128)S(1)}, f32[384,512]{1,0:T(8,128)S(1)}, u32[]{:S(2)}, u32[]{:S(2)}) collective-permute-start(f32[384,512]{1,0:T(8,128)S(1)} %get-tuple-element.62.mine_ref), channel_id=1, source_target_pairs={{0,8},{8,0},{1,9},{9,1},{2,10},{10,2},{3,11},{11,3},{4,12},{12,4},... | collective-permute-start | bytes 2359304 | tf_op jit(solution)/shard_map/ppermute | solution.py:363
  72.7 14.6 %collective-permute-start.13 = (f32[64,1536]{1,0:T(8,128)S(1)}, f32[64,1536]{1,0:T(8,128)S(1)}, u32[]{:S(2)}, u32[]{:S(2)}) collective-permute-start(f32[64,1536]{1,0:T(8,128)S(1)} %slice.18), channel_id=1, source_target_pairs={{0,2},{2,4},{4,6},{6,0},{1,3},{3,5},{5,7},{7,1},{8,10},{10,12},{12... | collective-permute-start | bytes 1179656 | tf_op jit(solution)/shard_map/ppermute | solution.py:363
  73.3 13.9 %collective-permute-start.14 = (f32[64,1536]{1,0:T(8,128)S(1)}, f32[64,1536]{1,0:T(8,128)S(1)}, u32[]{:S(2)}, u32[]{:S(2)}) collective-permute-start(f32[64,1536]{1,0:T(8,128)S(1)} %slice.19), channel_id=1, source_target_pairs={{0,6},{2,0},{4,2},{6,4},{1,7},{3,1},{5,3},{7,5},{8,14},{10,8},{12,... | collective-permute-start | bytes 1179656 | tf_op jit(solution)/shard_map/ppermute | solution.py:363
